TPU v7x, 32 devices: a whole 2x2x4 slice. The times are simulated.
32 devices in a mesh: parts: 2 (over y), fsdp: 8 (over z, x), clients: 2 (over core).
Axes of the slice: x: 2, y: 2, z: 4, core: 2. Of those that a mesh axis runs over, the one named last changes fastest.
Arguments:
- pool_x: bfloat16 [32768, 2560], P(('parts', 'fsdp')), parts along dimension 0, may hold values from -6 to 6
- pool_cot: bfloat16 [32768, 1024], P(('parts', 'fsdp')), parts along dimension 0, may hold values from -0.06591797 to 0.06591797
- assignment: int32 [16, 2048], P(('parts', 'fsdp'), 'clients'), parts along dimension 0, may hold values from 0 to 2047, each once within a row
- weight: float32 [2560, 1024], P('fsdp'), may hold values from -0.125 to 0.125
- gain: float32 [128], replicated, may hold values from 0.1 to 1.9
- global_variate: float32 [5120, 1024], P(('parts', 'fsdp')), parts along dimension 0, may hold values from -6 to 6
- client_variate: float32 [4, 2560, 1024], P(('parts', 'clients'), 'fsdp'), parts along dimension 0, may hold values from -6 to 6
Outputs:
- new_weight: float32 [5120, 1024], P(('parts', 'fsdp')), parts along dimension 0
- new_global: float32 [5120, 1024], P(('parts', 'fsdp')), parts along dimension 0
- new_client: float32 [4, 2560, 1024], P(('parts', 'clients'), 'fsdp'), parts along dimension 0
There are 2 independent parts, one for each index of `parts`. A program takes and returns all parts, laid end to end along the dimension named above; an argument that names none is the same for every part. Nothing has to cross between parts.
Inputs may be any that keep to these rules, and one draw needn't show every extreme that they name: Each row of assignment holds every local pool row index once.
All inputs are finite; a program needn't handle non-finite values.
Results may differ from a plain program's by a relative error of at most 0.0029.
Values may be sent and summed in bfloat16 or wider, within the bound.
A program may use at most 128 MiB of HBM per device.

v0:
```python
import jax
import jax.numpy as jnp
from jax import lax
from jax.sharding import PartitionSpec as P

KV_HEADS = 8
HEAD = 128


norm_eps = 1e-06
local_rate = 0.05


def norm_backward(keys, cotangent, gain):
    count = keys.shape[0]
    heads = keys.reshape(count, KV_HEADS, HEAD)
    inverse = lax.rsqrt(jnp.mean(heads * heads, axis=-1, keepdims=True) + norm_eps)
    scaled = cotangent.astype(jnp.float32).reshape(count, KV_HEADS, HEAD) * gain
    along = jnp.sum(scaled * heads, axis=-1, keepdims=True)
    result = scaled * inverse - heads * along * inverse * inverse * inverse / HEAD
    return result.reshape(count, KV_HEADS * HEAD).astype(jnp.bfloat16)


def per_device(pool_x, pool_cot, assignment, weight, gain, global_variate, client_variate):
    picked = assignment[0]
    x_rows = jnp.take(pool_x, picked, axis=0)
    cot_rows = jnp.take(pool_cot, picked, axis=0)
    weight_b = weight.astype(jnp.bfloat16)
    shard_rows = weight.shape[0]
    members = lax.axis_size("clients")
    half_rows = shard_rows // members
    own_half = lax.dynamic_slice_in_dim(
        weight_b, lax.axis_index("clients") * half_rows, half_rows, 0
    )
    columns = x_rows
    keys = jnp.dot(
        columns,
        lax.all_gather(own_half, ("fsdp", "clients"), axis=0, tiled=True),
        preferred_element_type=jnp.float32,
    )
    dkeys = norm_backward(keys, cot_rows, gain)
    own_variate = client_variate[0]
    columns = x_rows
    grads = lax.psum_scatter(
        lax.dot_general(
            columns, dkeys, (((0,), (0,)), ((), ())), preferred_element_type=jnp.float32
        ),
        "fsdp",
        scatter_dimension=0,
        tiled=True,
    )
    delta = -local_rate * (grads - own_variate + global_variate)
    change = grads - own_variate
    total_delta, total_change = lax.psum((delta, change), "clients")
    new_weight = weight + total_delta / members
    new_global = global_variate + total_change / members
    return (new_weight, new_global, grads[None])


def solution(mesh):
    placed = (
        P(("parts", "fsdp"), None),
        P(("parts", "fsdp"), None),
        P(("parts", "fsdp"), "clients"),
        P("fsdp", None),
        P(),
        P(("parts", "fsdp"), None),
        P(("parts", "clients"), "fsdp", None),
    )
    return jax.shard_map(
        per_device,
        mesh=mesh,
        in_specs=placed,
        out_specs=(
            P(("parts", "fsdp"), None),
            P(("parts", "fsdp"), None),
            P(("parts", "clients"), "fsdp", None),
        ),
        check_vma=False,
    )
```

profile of v0, /device:TPU:0, one launch (start us, length us, event | category | flops | bytes accessed | tf_op | source)
XLA Modules:
  0.0 303.5 jit_solution(13582425374234706983)
XLA Ops:
  7.2 0.0 all-gather.2.cloned.1.call-start
  7.2 1.9 dynamic-slice_convert_fusion
  9.1 0.0 all-gather.2.cloned.1.call-update
  9.1 0.0 reduce-scatter.2.cloned.1.call-start
  9.2 0.7 compare_select_fusion
  9.9 8.8 %gather_fusion.1 = bf16[1024,1024]{1,0:T(8,128)(2,1)} fusion(bf16[2048,1024]{1,0:T(8,128)(2,1)} %param.8, s32[1024]{0:T(1024)S(1)} %broadcast_clamp_fusion), kind=kCustom, calls=%fused_computation.1 | custom fusion | bytes 4198400 | tf_op jit(solution)/shard_map/jit(_take)/gather | solution.py:27
  18.6 2.9 copy.12
  21.5 0.0 copy-start.3
  21.5 0.0 copy-start.2
  21.5 15.9 %gather_fusion = bf16[1024,2560]{1,0:T(8,128)(2,1)} fusion(bf16[2048,2560]{1,0:T(8,128)(2,1)} %param.7, s32[1024]{0:T(1024)S(1)} %broadcast_clamp_fusion), kind=kCustom, calls=%fused_computation | custom fusion | bytes 10489856 | tf_op jit(solution)/shard_map/jit(_take)/gather | solution.py:26
  37.4 32.1 %all-gather.2.cloned.1.call-done = bf16[2560,1024]{1,0:T(8,128)(2,1)} async-done(((bf16[160,1024]{1,0:T(8,128)(2,1)}), bf16[2560,1024]{1,0:T(8,128)(2,1)}) %all-gather.2.cloned.1.call-update) | async-done | bytes 5242896 | tf_op jit(solution)/shard_map/all_gather | solution.py:38
  69.6 9.4 %multiply_reduce_fusion.1 = (f32[1024,8]{0,1:T(8,128)S(1)}, f32[1024,1024]{0,1:T(8,128)S(1)}) fusion(bf16[2560,1024]{1,0:T(8,128)(2,1)} %all-gather.2.cloned.1.call-done, bf16[1024,2560]{1,0:T(8,128)(2,1)} %gather_fusion, pred[1024]{0:T(1024)(128)(4,1)S(1)} %compare_and_fusion), kind=kOutput, calls=%fused_computation.15 | convolution fusion | flops 5373419520 | bytes 14713856 | tf_op jit(solution)/shard_map/dot_general | solution.py:36
  79.0 0.0 slice-start
  79.0 0.9 fusion
  79.9 2.3 fusion.2
  82.3 9.0 %fusion.5 = f32[2560,1024]{1,0:T(8,128)} fusion(bf16[1024,1024]{0,1:T(8,128)(2,1)S(1)} %fusion.2, bf16[1024,2560]{1,0:T(8,128)(2,1)S(1)} %bitcast.41, pred[1024]{0:T(1024)(128)(4,1)S(1)} %compare_and_fusion), kind=kOutput, calls=%fused_computation.16 | convolution fusion | flops 5371330560 | bytes 17826816 | tf_op jit(solution)/shard_map/dot_general | solution.py:45
  91.2 0.0 reduce-scatter.2.cloned.1.call-update
  91.2 0.0 copy-start.1
  91.3 0.0 all-reduce.3.cloned.1.call-start
  91.3 176.8 %reduce-scatter.2.cloned.1.call-done = f32[320,1024]{1,0:T(8,128)} async-done(((f32[2560,1024]{1,0:T(8,128)}), f32[320,1024]{1,0:T(8,128)}) %reduce-scatter.2.cloned.1.call-update) | async-done | bytes 1310736 | tf_op jit(solution)/shard_map/reduce_scatter | solution.py:44
  268.1 3.7 %add_multiply_fusion = (f32[320,1024]{1,0:T(8,128)}, f32[320,1024]{1,0:T(8,128)}) fusion(f32[320,1024]{1,0:T(8,128)S(1)} %copy-done, f32[320,1024]{1,0:T(8,128)} %reduce-scatter.2.cloned.1.call-done, f32[1,320,1024]{2,1,0:T(8,128)} %param.13), kind=kLoop, calls=%fused_computation.23 | loop fusion | flops 983040 | bytes 6553600 | tf_op jit(solution)/shard_map/mul | solution.py:52
  271.8 0.0 all-reduce.3.cloned.1.call-update
  271.8 21.5 %all-reduce.3.cloned.1.call-done = (f32[320,1024]{1,0:T(8,128)}, f32[320,1024]{1,0:T(8,128)}) async-done(((f32[320,1024]{1,0:T(8,128)}, f32[320,1024]{1,0:T(8,128)}), (f32[320,1024]{1,0:T(8,128)}, f32[320,1024]{1,0:T(8,128)})) %all-reduce.3.cloned.1.call-update) | async-done | bytes 2621456 | tf_op jit(solution)/shard_map/psum | solution.py:54
  293.3 3.8 %multiply_add_fusion = (f32[320,1024]{1,0:T(8,128)}, f32[320,1024]{1,0:T(8,128)}) fusion(f32[320,1024]{1,0:T(8,128)S(1)} %copy-done, f32[320,1024]{1,0:T(8,128)} %get-tuple-element.4, f32[320,1024]{1,0:T(8,128)S(1)} %copy-done.1, f32[320,1024]{1,0:T(8,128)} %get-tuple-element.3), kind=kLoop, calls=%fused_computation.21 | loop fusion | flops 1310720 | bytes 7864320 | tf_op jit(solution)/shard_map/add | solution.py:56
  (13 shorter events, 0.0 us)
Async XLA Ops:
  7.2 62.4 %all-gather.2.cloned.1.call-start = ((), (), s32[]{:S(2)}) async-start(), calls=%async_computation.1 | async-start | bytes 5570560 | tf_op jit(solution)/shard_map/all_gather | solution.py:38
  9.1 259.0 %reduce-scatter.2.cloned.1.call-start = ((), (), s32[]{:S(2)}) async-start(), calls=%async_computation.2 | async-start | bytes 11796480 | tf_op jit(solution)/shard_map/reduce_scatter | solution.py:44
  21.5 15.9 %copy-start.3 = (f32[128]{0:T(128)S(1)}, f32[128]{0:T(128)}, u32[]{:S(2)}) copy-start(f32[128]{0:T(128)} %param.11) | copy-start | bytes 1540
  21.5 15.9 %copy-start.2 = (s32[1,1024]{1,0:T(1,128)S(1)}, s32[1,1024]{1,0:T(1,128)}, u32[]{:S(2)}) copy-start(s32[1,1024]{1,0:T(1,128)} %param.9) | copy-start | bytes 12292
  79.0 3.2 %slice-start = ((s8[5242880]{0:T(1024)(128)(4,1)}), s8[4194304]{0:T(1024)(128)(4,1)S(1)}, s32[]{:S(2)}) async-start(s8[5242880]{0:T(1024)(128)(4,1)} %bitcast.40), calls=%async_computation.4 | async-start | bytes 8388608
  79.9 2.3 slice-start.1
  91.2 176.8 %copy-start = (f32[320,1024]{1,0:T(8,128)S(1)}, f32[320,1024]{1,0:T(8,128)}, u32[]{:S(2)}) copy-start(f32[320,1024]{1,0:T(8,128)} %param.12) | copy-start | bytes 3932164
  91.2 202.0 %copy-start.1 = (f32[320,1024]{1,0:T(8,128)S(1)}, f32[320,1024]{1,0:T(8,128)}, u32[]{:S(2)}) copy-start(f32[320,1024]{1,0:T(8,128)} %param.10) | copy-start | bytes 3932164
  91.3 202.0 %all-reduce.3.cloned.1.call-start = ((), (), s32[]{:S(2)}) async-start(), calls=%async_computation.3 | async-start | bytes 5242880 | tf_op jit(solution)/shard_map/psum | solution.py:54
Sparse Core Ops, SparseCore 0:
  10.9 58.6 all-gather.1
  91.4 176.6 reduce-scatter.1
  271.9 21.3 all-reduce.2
where the time goes:
time: 304 us
  waiting for transfers between devices  230 us (76%)
  local copies, waits for them, and re-layouts  29.4 us (10%)
  matrix products  18.4 us (6%)
  between operations  13.9 us (5%)
  other arithmetic  11.4 us (4%)
    reduce_scatter x1, waiting for transfers between devices, per_device(): lax.psum_scatter(lax.dot_general(columns, dkeys, (((0,), (0,)), ((), ()))...  177 us
    all_gather x1, waiting for transfers between devices, per_device(): lax.all_gather(own_half, ('fsdp', 'clients'), axis=0, tiled=True)  32.1 us
    psum x1, waiting for transfers between devices, per_device(): total_delta, total_change = lax.psum((delta, change), 'clients')  21.5 us
    gather x1, local copies, waits for them, and re-layouts, per_device(): x_rows = jnp.take(pool_x, picked, axis=0)  15.9 us
    gather x2, local copies, waits for them, and re-layouts, per_device(): cot_rows = jnp.take(pool_cot, picked, axis=0)  11.7 us
    dot_general x1, matrix products, per_device(): jnp.dot(columns, lax.all_gather(own_half, ('fsdp', 'clients'), axis=0, ti...  9.4 us
    dot_general x1, matrix products, per_device(): lax.dot_general(columns, dkeys, (((0,), (0,)), ((), ())), preferred_eleme...  8.96 us
  transfers between devices with their start and end apart: 3, of which 3 were waited for; matrix products, arithmetic and copies ran while one was open for 9% of the time, Pallas kernels for 0%

commit v1 on v0

v1 whole, which is shorter than its diff:
```python
import jax
import jax.numpy as jnp
from jax import lax
from jax.sharding import PartitionSpec as P

HEAD = 128

norm_eps = 1e-06
local_rate = 0.05
CHUNKS = 4


def norm_backward(keys, cotangent, gain):
    count, width = keys.shape
    heads = keys.reshape(count, width // HEAD, HEAD)
    inverse = lax.rsqrt(jnp.mean(heads * heads, axis=-1, keepdims=True) + norm_eps)
    scaled = cotangent.astype(jnp.float32).reshape(heads.shape) * gain
    along = jnp.sum(scaled * heads, axis=-1, keepdims=True)
    result = scaled * inverse - heads * along * inverse * inverse * inverse / HEAD
    return result.reshape(count, width).astype(jnp.bfloat16)


def gather_weight(weight):
    weight_b = weight.astype(jnp.bfloat16)
    members = lax.axis_size("clients")
    parts = lax.axis_size("parts")
    rows = weight.shape[0] // (members * parts)
    place = lax.axis_index("clients") * parts + lax.axis_index("parts")
    own = lax.dynamic_slice_in_dim(weight_b, place * rows, rows, 0)
    return lax.all_gather(own, ("fsdp", "clients", "parts"), axis=0, tiled=True)


def scatter_sum(partial):
    n = lax.axis_size("fsdp")
    lines = n // 2
    me = lax.axis_index("fsdp")
    line, side = me // 2, lax.rem(me, 2)
    rows = partial.shape[0] // n
    blocks = partial.reshape(lines, 2, rows, partial.shape[1])
    away = lax.dynamic_index_in_dim(blocks, 1 - side, 1, keepdims=False)
    home = lax.dynamic_index_in_dim(blocks, side, 1, keepdims=False)
    came = lax.ppermute(
        away.astype(jnp.bfloat16), "fsdp", [(i, i ^ 1) for i in range(n)]
    )
    both = home + came.astype(jnp.float32)
    own = lax.dynamic_index_in_dim(both, line, 0, keepdims=False)
    if lines <= 4:
        total = own
        for step in range(1, lines):
            block = lax.dynamic_index_in_dim(
                both, lax.rem(line + step, lines), 0, keepdims=False
            )
            pairs = [(i, (i + 2 * step) % n) for i in range(n)]
            got = lax.ppermute(block.astype(jnp.bfloat16), "fsdp", pairs)
            total = total + got.astype(jnp.float32)
        return total
    groups = [[2 * z + x for z in range(lines)] for x in range(2)]
    got = lax.all_to_all(
        both.astype(jnp.bfloat16), "fsdp", 0, 0, axis_index_groups=groups
    ).astype(jnp.float32)
    others = jnp.arange(lines)[:, None, None] != line
    return own + jnp.sum(jnp.where(others, got, 0.0), axis=0)


def per_device(pool_x, pool_cot, assignment, weight, gain, global_variate, client_variate):
    members = lax.axis_size("clients")
    weight_b = gather_weight(weight)
    picked = assignment[0]
    x_rows = jnp.take(pool_x, picked, axis=0)
    cot_rows = jnp.take(pool_cot, picked, axis=0)
    width = weight.shape[1] // CHUNKS
    own_variate = client_variate[0]
    results = []
    for chunk in range(CHUNKS):
        cut = slice(chunk * width, (chunk + 1) * width)
        keys = jnp.dot(x_rows, weight_b[:, cut], preferred_element_type=jnp.float32)
        dkeys = norm_backward(keys, cot_rows[:, cut], gain)
        partial = lax.dot_general(
            x_rows, dkeys, (((0,), (0,)), ((), ())), preferred_element_type=jnp.float32
        )
        grads = scatter_sum(partial)
        change = grads - own_variate[:, cut]
        total_change = change
        for step in range(1, members):
            pairs = [(i, (i + step) % members) for i in range(members)]
            total_change = total_change + lax.ppermute(change, "clients", pairs)
        common = global_variate[:, cut]
        total_delta = -local_rate * (total_change + members * common)
        new_weight = weight[:, cut] + total_delta / members
        new_global = common + total_change / members
        results.append((new_weight, new_global, grads))
    new_weight, new_global, grads = (
        jnp.concatenate(list(pieces), axis=1) for pieces in zip(*results)
    )
    return (new_weight, new_global, grads[None])


def solution(mesh):
    placed = (
        P(("parts", "fsdp"), None),
        P(("parts", "fsdp"), None),
        P(("parts", "fsdp"), "clients"),
        P("fsdp", None),
        P(),
        P(("parts", "fsdp"), None),
        P(("parts", "clients"), "fsdp", None),
    )
    return jax.shard_map(
        per_device,
        mesh=mesh,
        in_specs=placed,
        out_specs=(
            P(("parts", "fsdp"), None),
            P(("parts", "fsdp"), None),
            P(("parts", "clients"), "fsdp", None),
        ),
        check_vma=False,
    )
```

time: 304 us -> 214 us (0.70)
  waiting for transfers between devices: 230 us -> 95.5 us
  starting transfers between devices: 0.12 us -> 27 us
  local copies, waits for them, and re-layouts: 29.4 us -> 37.9 us
  other arithmetic: 11.4 us -> 17.5 us
    reduce_scatter x1 -> x0, waiting for transfers between devices: 177 us -> none  [per_device(): lax.psum_scatter(lax.dot_general(columns, dkeys, (((0,), (0,)), ((), ()))...]
    ppermute x0 -> x20, waiting for transfers between devices: none -> 69.2 us  [the longest x4 43.8 us: scatter_sum(): lax.ppermute(away.astype(jnp.bfloat16), 'fsdp', [(i, i ^ 1) for i in rang...]
    ppermute x0 -> x20, starting transfers between devices: none -> 27 us  [the longest x12 22 us: scatter_sum(): got = lax.ppermute(block.astype(jnp.bfloat16), 'fsdp', pairs)]
    psum x1 -> x0, waiting for transfers between devices: 21.5 us -> none  [per_device(): total_delta, total_change = lax.psum((delta, change), 'clients')]
    select_n x0 -> x1, local copies, waits for them, and re-layouts: none -> 7.96 us  [per_device(): x_rows = jnp.take(pool_x, picked, axis=0)]
    all_gather x1, waiting for transfers between devices: 32.1 us -> 26.2 us  [gather_weight(): return lax.all_gather(own, ('fsdp', 'clients', 'parts'), axis=0, tiled=True)]
    select_n x1 -> x2, other arithmetic: 0.69 us -> 6 us  [per_device(): x_rows = jnp.take(pool_x, picked, axis=0)]
    mul x1 -> x0, other arithmetic: 3.7 us -> none  [per_device(): delta = -local_rate * (grads - own_variate + global_variate)]
  transfers between devices with their start and end apart: 3 -> 21, of which waited for: 3 -> 10; matrix products, arithmetic and copies ran while one was open for 9% -> 24% of each run, Pallas kernels for 0% -> 0%
where the time goes in v1:
time: 214 us; the launch traced here: 212 us
  waiting for transfers between devices  95.5 us (45%)
  local copies, waits for them, and re-layouts  37.9 us (18%)
  starting transfers between devices  27 us (13%)
  matrix products  19.8 us (9%)
  other arithmetic  17.5 us (8%)
  between operations  14.5 us (7%)
    ppermute x4, waiting for transfers between devices, scatter_sum(): lax.ppermute(away.astype(jnp.bfloat16), 'fsdp', [(i, i ^ 1) for i in rang...  43.8 us
    all_gather x1, waiting for transfers between devices, gather_weight(): return lax.all_gather(own, ('fsdp', 'clients', 'parts'), axis=0, tiled=True)  26.2 us
    ppermute x12, waiting for transfers between devices, scatter_sum(): got = lax.ppermute(block.astype(jnp.bfloat16), 'fsdp', pairs)  24.8 us
    ppermute x12, starting transfers between devices, scatter_sum(): got = lax.ppermute(block.astype(jnp.bfloat16), 'fsdp', pairs)  22 us
    gather x1, local copies, waits for them, and re-layouts, per_device(): x_rows = jnp.take(pool_x, picked, axis=0)  15.8 us
    dot_general x4, matrix products, per_device(): keys = jnp.dot(x_rows, weight_b[:, cut], preferred_element_type=jnp.float32)  12.8 us
    gather x2, local copies, waits for them, and re-layouts, per_device(): cot_rows = jnp.take(pool_cot, picked, axis=0)  10.3 us
    select_n x1, local copies, waits for them, and re-layouts, per_device(): x_rows = jnp.take(pool_x, picked, axis=0)  7.96 us
  transfers between devices with their start and end apart: 21, of which 10 were waited for; matrix products, arithmetic and copies ran while one was open for 24% of the time, Pallas kernels for 0%

profile of v1, /device:TPU:0, one launch (start us, length us, event | category | flops | bytes accessed | tf_op | source)
XLA Modules:
  0.0 212.2 jit_solution(8543625039180659123)
XLA Ops:
  9.7 15.8 %gather_fusion = bf16[1024,2560]{1,0:T(8,128)(2,1)} fusion(bf16[2048,2560]{1,0:T(8,128)(2,1)} %param.7, s32[1024]{0:T(1024)S(1)} %broadcast_clamp_fusion), kind=kCustom, calls=%fused_computation | custom fusion | bytes 10489856 | tf_op jit(solution)/shard_map/jit(_take)/gather | solution.py:69
  25.4 7.7 %gather_fusion.1 = bf16[1024,1024]{1,0:T(8,128)(2,1)S(1)} fusion(bf16[2048,1024]{1,0:T(8,128)(2,1)} %param.8, s32[1024]{0:T(1024)S(1)} %broadcast_clamp_fusion), kind=kCustom, calls=%fused_computation.1 | custom fusion | bytes 4198400 | tf_op jit(solution)/shard_map/jit(_take)/gather | solution.py:70
  33.2 2.6 %copy.23 = bf16[1024,1024]{0,1:T(8,128)(2,1)} copy(bf16[1024,1024]{1,0:T(8,128)(2,1)S(1)} %gather_fusion.1) | data formatting | bytes 4194304 | tf_op jit(solution)/shard_map/jit(_take)/gather | solution.py:70
  35.8 5.3 %fusion.68 = bf16[2560,1024]{0,1:T(8,128)(2,1)} fusion(bf16[1024,2560]{1,0:T(8,128)(2,1)} %gather_fusion, pred[1024]{0:T(1024)(128)(4,1)S(1)} %compare_and_fusion), kind=kLoop, calls=%fused_computation.153 | loop fusion | flops 2621440 | bytes 10486784 | tf_op jit(solution)/shard_map/jit(_take)/select_n | solution.py:69
  41.1 8.0 %copy.22 = bf16[2560,1024]{1,0:T(8,128)(2,1)} copy(bf16[2560,1024]{0,1:T(8,128)(2,1)} %fusion.68) | data formatting | bytes 10485760 | tf_op jit(solution)/shard_map/jit(_take)/select_n | solution.py:69
  50.9 1.9 slice_convert_fusion.3
  52.7 26.2 %all-gather.2.cloned.1.call-done = bf16[2560,1024]{1,0:T(8,128)(2,1)} async-done(((bf16[80,1024]{1,0:T(8,128)(2,1)}), bf16[2560,1024]{1,0:T(8,128)(2,1)}) %all-gather.2.cloned.1.call-update) | async-done | bytes 5242896 | tf_op jit(solution)/shard_map/all_gather | solution.py:30
  79.0 4.7 %multiply_reduce_fusion.3 = (f32[1024,2]{0,1:T(2,128)S(1)}, f32[1024,256]{0,1:T(8,128)S(1)}) fusion(bf16[2560,1024]{1,0:T(8,128)(2,1)} %all-gather.2.cloned.1.call-done, bf16[1024,2560]{1,0:T(8,128)(2,1)} %gather_fusion, pred[1024]{0:T(1024)(128)(4,1)S(1)} %compare_and_fusion), kind=kOutput, calls=%fused_computation.64 | convolution fusion | flops 1345320960 | bytes 7611392 | tf_op jit(solution)/shard_map/dot_general | solution.py:76
  83.7 4.3 %multiply_reduce_fusion.1 = (f32[1024,2]{0,1:T(2,128)S(1)}, f32[1024,256]{0,1:T(8,128)S(1)}) fusion(bf16[2560,1024]{1,0:T(8,128)(2,1)S(1)} %copy-done.8, bf16[1024,2560]{1,0:T(8,128)(2,1)} %gather_fusion, pred[1024]{0:T(1024)(128)(4,1)S(1)} %compare_and_fusion), kind=kOutput, calls=%fused_computation.61 | convolution fusion | flops 1345320960 | bytes 7611392 | tf_op jit(solution)/shard_map/dot_general | solution.py:76
  90.0 1.8 multiply_reduce_fusion.5
  99.6 1.9 fusion.38
  108.0 21.8 %collective-permute-done.10 = bf16[4,320,256]{2,1,0:T(8,128)(2,1)S(1)} collective-permute-done((bf16[4,320,256]{2,1,0:T(8,128)(2,1)S(1)}, bf16[4,320,256]{2,1,0:T(8,128)(2,1)S(1)}, u32[]{:S(2)}, u32[]{:S(2)}) %collective-permute-start.10) | collective-permute-done | bytes 655392 | tf_op jit(solution)/shard_map/ppermute | solution.py:42
  130.0 2.0 collective-permute-start.11
  132.8 11.0 %collective-permute-done.15 = bf16[4,320,256]{2,1,0:T(8,128)(2,1)S(1)} collective-permute-done((bf16[4,320,256]{2,1,0:T(8,128)(2,1)S(1)}, bf16[4,320,256]{2,1,0:T(8,128)(2,1)S(1)}, u32[]{:S(2)}, u32[]{:S(2)}) %collective-permute-start.15) | collective-permute-done | bytes 655392 | tf_op jit(solution)/shard_map/ppermute | solution.py:42
  143.8 2.2 %collective-permute-start.13 = (bf16[320,256]{1,0:T(8,128)(2,1)S(1)}, bf16[320,256]{1,0:T(8,128)(2,1)S(1)}, u32[]{:S(2)}, u32[]{:S(2)}) collective-permute-start(bf16[320,256]{1,0:T(8,128)(2,1)S(1)} %get-tuple-element.37), channel_id=1, source_target_pairs={{0,12},{2,14},{4,0},{6,2},{8,4},{10,6},{12,8},{14,10},{1,13},{3,15... | collective-permute-start | bytes 491528 | tf_op jit(solution)/shard_map/ppermute | solution.py:54
  146.2 11.0 %collective-permute-done = bf16[4,320,256]{2,1,0:T(8,128)(2,1)S(1)} collective-permute-done((bf16[4,320,256]{2,1,0:T(8,128)(2,1)S(1)}, bf16[4,320,256]{2,1,0:T(8,128)(2,1)S(1)}, u32[]{:S(2)}, u32[]{:S(2)}) %collective-permute-start) | collective-permute-done | bytes 655392 | tf_op jit(solution)/shard_map/ppermute | solution.py:42
  157.2 1.9 collective-permute-start.16
  160.3 2.4 %collective-permute-start.18 = (bf16[320,256]{1,0:T(8,128)(2,1)S(1)}, bf16[320,256]{1,0:T(8,128)(2,1)S(1)}, u32[]{:S(2)}, u32[]{:S(2)}) collective-permute-start(bf16[320,256]{1,0:T(8,128)(2,1)S(1)} %get-tuple-element.40), channel_id=1, source_target_pairs={{0,12},{2,14},{4,0},{6,2},{8,4},{10,6},{12,8},{14,10},{1,13},{3,15... | collective-permute-start | bytes 491528 | tf_op jit(solution)/shard_map/ppermute | solution.py:54
  166.7 10.4 %collective-permute-done.17 = bf16[320,256]{1,0:T(8,128)(2,1)S(1)} collective-permute-done((bf16[320,256]{1,0:T(8,128)(2,1)S(1)}, bf16[320,256]{1,0:T(8,128)(2,1)S(1)}, u32[]{:S(2)}, u32[]{:S(2)}) %collective-permute-start.17) | collective-permute-done | bytes 163872 | tf_op jit(solution)/shard_map/ppermute | solution.py:54
  177.2 3.8 %collective-permute-start.6 = (bf16[320,256]{1,0:T(8,128)(2,1)S(1)}, bf16[320,256]{1,0:T(8,128)(2,1)S(1)}, u32[]{:S(2)}, u32[]{:S(2)}) collective-permute-start(bf16[320,256]{1,0:T(8,128)(2,1)S(1)} %get-tuple-element.33), channel_id=1, source_target_pairs={{0,4},{2,6},{4,8},{6,10},{8,12},{10,14},{12,0},{14,2},{1,5},{3,7},... | collective-permute-start | bytes 491528 | tf_op jit(solution)/shard_map/ppermute | solution.py:54
  181.0 3.9 %collective-permute-start.7 = (bf16[320,256]{1,0:T(8,128)(2,1)S(1)}, bf16[320,256]{1,0:T(8,128)(2,1)S(1)}, u32[]{:S(2)}, u32[]{:S(2)}) collective-permute-start(bf16[320,256]{1,0:T(8,128)(2,1)S(1)} %get-tuple-element.35), channel_id=1, source_target_pairs={{0,8},{2,10},{4,12},{6,14},{8,0},{10,2},{12,4},{14,6},{1,9},{3,11}... | collective-permute-start | bytes 491528 | tf_op jit(solution)/shard_map/ppermute | solution.py:54
  184.8 2.0 collective-permute-start.8
  186.9 5.9 %collective-permute-done.2 = bf16[320,256]{1,0:T(8,128)(2,1)S(1)} collective-permute-done((bf16[320,256]{1,0:T(8,128)(2,1)S(1)}, bf16[320,256]{1,0:T(8,128)(2,1)S(1)}, u32[]{:S(2)}, u32[]{:S(2)}) %collective-permute-start.2) | collective-permute-done | bytes 163872 | tf_op jit(solution)/shard_map/ppermute | solution.py:54
  193.2 6.6 %collective-permute-done.7 = bf16[320,256]{1,0:T(8,128)(2,1)S(1)} collective-permute-done((bf16[320,256]{1,0:T(8,128)(2,1)S(1)}, bf16[320,256]{1,0:T(8,128)(2,1)S(1)}, u32[]{:S(2)}, u32[]{:S(2)}) %collective-permute-start.7) | collective-permute-done | bytes 163872 | tf_op jit(solution)/shard_map/ppermute | solution.py:54
  (93 shorter events, 32.5 us)
Async XLA Ops:
  7.2 71.8 %all-gather.2.cloned.1.call-start = ((), (), s32[]{:S(2)}) async-start(), calls=%async_computation | async-start | bytes 5406720 | tf_op jit(solution)/shard_map/all_gather | solution.py:30
  79.0 9.2 %slice-start = ((s8[5242880]{0:T(1024)(128)(4,1)}), s8[4194304]{0:T(1024)(128)(4,1)S(1)}, s32[]{:S(2)}) async-start(s8[5242880]{0:T(1024)(128)(4,1)} %bitcast.212), calls=%async_computation.1 | async-start | bytes 8388608
  98.1 61.3 %collective-permute-start.5 = (bf16[4,320,256]{2,1,0:T(8,128)(2,1)S(1)}, bf16[4,320,256]{2,1,0:T(8,128)(2,1)S(1)}, u32[]{:S(2)}, u32[]{:S(2)}) collective-permute-start(bf16[4,320,256]{2,1,0:T(8,128)(2,1)S(1)} %fusion.33), channel_id=1, source_target_pairs={{0,2},{2,0},{4,6},{6,4},{8,10},{10,8},{12,14},{14,12},{1,3},{3,1},... | collective-permute-start | bytes 1966088 | tf_op jit(solution)/shard_map/ppermute | solution.py:42
  101.6 28.2 %collective-permute-start.10 = (bf16[4,320,256]{2,1,0:T(8,128)(2,1)S(1)}, bf16[4,320,256]{2,1,0:T(8,128)(2,1)S(1)}, u32[]{:S(2)}, u32[]{:S(2)}) collective-permute-start(bf16[4,320,256]{2,1,0:T(8,128)(2,1)S(1)} %fusion.34), channel_id=1, source_target_pairs={{0,2},{2,0},{4,6},{6,4},{8,10},{10,8},{12,14},{14,12},{1,3},{3,1},... | collective-permute-start | bytes 1966088 | tf_op jit(solution)/shard_map/ppermute | solution.py:42
  104.1 39.8 %collective-permute-start.15 = (bf16[4,320,256]{2,1,0:T(8,128)(2,1)S(1)}, bf16[4,320,256]{2,1,0:T(8,128)(2,1)S(1)}, u32[]{:S(2)}, u32[]{:S(2)}) collective-permute-start(bf16[4,320,256]{2,1,0:T(8,128)(2,1)S(1)} %fusion.35), channel_id=1, source_target_pairs={{0,2},{2,0},{4,6},{6,4},{8,10},{10,8},{12,14},{14,12},{1,3},{3,1},... | collective-permute-start | bytes 1966088 | tf_op jit(solution)/shard_map/ppermute | solution.py:42
  107.3 49.9 %collective-permute-start = (bf16[4,320,256]{2,1,0:T(8,128)(2,1)S(1)}, bf16[4,320,256]{2,1,0:T(8,128)(2,1)S(1)}, u32[]{:S(2)}, u32[]{:S(2)}) collective-permute-start(bf16[4,320,256]{2,1,0:T(8,128)(2,1)S(1)} %fusion.32), channel_id=1, source_target_pairs={{0,2},{2,0},{4,6},{6,4},{8,10},{10,8},{12,14},{14,12},{1,3},{3,1},... | collective-permute-start | bytes 1966088 | tf_op jit(solution)/shard_map/ppermute | solution.py:42
  130.0 30.3 %collective-permute-start.11 = (bf16[320,256]{1,0:T(8,128)(2,1)S(1)}, bf16[320,256]{1,0:T(8,128)(2,1)S(1)}, u32[]{:S(2)}, u32[]{:S(2)}) collective-permute-start(bf16[320,256]{1,0:T(8,128)(2,1)S(1)} %get-tuple-element.36), channel_id=1, source_target_pairs={{0,4},{2,6},{4,8},{6,10},{8,12},{10,14},{12,0},{14,2},{1,5},{3,7},... | collective-permute-start | bytes 491528 | tf_op jit(solution)/shard_map/ppermute | solution.py:54
  132.0 30.7 %collective-permute-start.12 = (bf16[320,256]{1,0:T(8,128)(2,1)S(1)}, bf16[320,256]{1,0:T(8,128)(2,1)S(1)}, u32[]{:S(2)}, u32[]{:S(2)}) collective-permute-start(bf16[320,256]{1,0:T(8,128)(2,1)S(1)} %get-tuple-element.38), channel_id=1, source_target_pairs={{0,8},{2,10},{4,12},{6,14},{8,0},{10,2},{12,4},{14,6},{1,9},{3,11}... | collective-permute-start | bytes 491528 | tf_op jit(solution)/shard_map/ppermute | solution.py:54
  143.8 18.8 %collective-permute-start.13 = (bf16[320,256]{1,0:T(8,128)(2,1)S(1)}, bf16[320,256]{1,0:T(8,128)(2,1)S(1)}, u32[]{:S(2)}, u32[]{:S(2)}) collective-permute-start(bf16[320,256]{1,0:T(8,128)(2,1)S(1)} %get-tuple-element.37), channel_id=1, source_target_pairs={{0,12},{2,14},{4,0},{6,2},{8,4},{10,6},{12,8},{14,10},{1,13},{3,15... | collective-permute-start | bytes 491528 | tf_op jit(solution)/shard_map/ppermute | solution.py:54
  157.2 9.0 %collective-permute-start.16 = (bf16[320,256]{1,0:T(8,128)(2,1)S(1)}, bf16[320,256]{1,0:T(8,128)(2,1)S(1)}, u32[]{:S(2)}, u32[]{:S(2)}) collective-permute-start(bf16[320,256]{1,0:T(8,128)(2,1)S(1)} %get-tuple-element.39), channel_id=1, source_target_pairs={{0,4},{2,6},{4,8},{6,10},{8,12},{10,14},{12,0},{14,2},{1,5},{3,7},... | collective-permute-start | bytes 491528 | tf_op jit(solution)/shard_map/ppermute | solution.py:54
  159.4 17.8 %collective-permute-start.17 = (bf16[320,256]{1,0:T(8,128)(2,1)S(1)}, bf16[320,256]{1,0:T(8,128)(2,1)S(1)}, u32[]{:S(2)}, u32[]{:S(2)}) collective-permute-start(bf16[320,256]{1,0:T(8,128)(2,1)S(1)} %get-tuple-element.41), channel_id=1, source_target_pairs={{0,8},{2,10},{4,12},{6,14},{8,0},{10,2},{12,4},{14,6},{1,9},{3,11}... | collective-permute-start | bytes 491528 | tf_op jit(solution)/shard_map/ppermute | solution.py:54
  160.3 20.7 %collective-permute-start.18 = (bf16[320,256]{1,0:T(8,128)(2,1)S(1)}, bf16[320,256]{1,0:T(8,128)(2,1)S(1)}, u32[]{:S(2)}, u32[]{:S(2)}) collective-permute-start(bf16[320,256]{1,0:T(8,128)(2,1)S(1)} %get-tuple-element.40), channel_id=1, source_target_pairs={{0,12},{2,14},{4,0},{6,2},{8,4},{10,6},{12,8},{14,10},{1,13},{3,15... | collective-permute-start | bytes 491528 | tf_op jit(solution)/shard_map/ppermute | solution.py:54
  162.6 22.2 %collective-permute-start.1 = (bf16[320,256]{1,0:T(8,128)(2,1)S(1)}, bf16[320,256]{1,0:T(8,128)(2,1)S(1)}, u32[]{:S(2)}, u32[]{:S(2)}) collective-permute-start(bf16[320,256]{1,0:T(8,128)(2,1)S(1)} %get-tuple-element.30), channel_id=1, source_target_pairs={{0,4},{2,6},{4,8},{6,10},{8,12},{10,14},{12,0},{14,2},{1,5},{3,7},... | collective-permute-start | bytes 491528 | tf_op jit(solution)/shard_map/ppermute | solution.py:54
  162.6 30.2 %collective-permute-start.2 = (bf16[320,256]{1,0:T(8,128)(2,1)S(1)}, bf16[320,256]{1,0:T(8,128)(2,1)S(1)}, u32[]{:S(2)}, u32[]{:S(2)}) collective-permute-start(bf16[320,256]{1,0:T(8,128)(2,1)S(1)} %get-tuple-element.32), channel_id=1, source_target_pairs={{0,8},{2,10},{4,12},{6,14},{8,0},{10,2},{12,4},{14,6},{1,9},{3,11}... | collective-permute-start | bytes 491528 | tf_op jit(solution)/shard_map/ppermute | solution.py:54
  166.2 26.6 %copy-start.5 = (f32[1,320,1024]{2,1,0:T(8,128)S(1)}, f32[1,320,1024]{2,1,0:T(8,128)}, u32[]{:S(2)}) copy-start(f32[1,320,1024]{2,1,0:T(8,128)} %param.13) | copy-start | bytes 3932164
  166.2 26.5 %collective-permute-start.3 = (bf16[320,256]{1,0:T(8,128)(2,1)S(1)}, bf16[320,256]{1,0:T(8,128)(2,1)S(1)}, u32[]{:S(2)}, u32[]{:S(2)}) collective-permute-start(bf16[320,256]{1,0:T(8,128)(2,1)S(1)} %get-tuple-element.31), channel_id=1, source_target_pairs={{0,12},{2,14},{4,0},{6,2},{8,4},{10,6},{12,8},{14,10},{1,13},{3,15... | collective-permute-start | bytes 491528 | tf_op jit(solution)/shard_map/ppermute | solution.py:54
  177.2 16.0 %collective-permute-start.6 = (bf16[320,256]{1,0:T(8,128)(2,1)S(1)}, bf16[320,256]{1,0:T(8,128)(2,1)S(1)}, u32[]{:S(2)}, u32[]{:S(2)}) collective-permute-start(bf16[320,256]{1,0:T(8,128)(2,1)S(1)} %get-tuple-element.33), channel_id=1, source_target_pairs={{0,4},{2,6},{4,8},{6,10},{8,12},{10,14},{12,0},{14,2},{1,5},{3,7},... | collective-permute-start | bytes 491528 | tf_op jit(solution)/shard_map/ppermute | solution.py:54
  181.0 18.8 %collective-permute-start.7 = (bf16[320,256]{1,0:T(8,128)(2,1)S(1)}, bf16[320,256]{1,0:T(8,128)(2,1)S(1)}, u32[]{:S(2)}, u32[]{:S(2)}) collective-permute-start(bf16[320,256]{1,0:T(8,128)(2,1)S(1)} %get-tuple-element.35), channel_id=1, source_target_pairs={{0,8},{2,10},{4,12},{6,14},{8,0},{10,2},{12,4},{14,6},{1,9},{3,11}... | collective-permute-start | bytes 491528 | tf_op jit(solution)/shard_map/ppermute | solution.py:54
  184.8 15.0 %collective-permute-start.8 = (bf16[320,256]{1,0:T(8,128)(2,1)S(1)}, bf16[320,256]{1,0:T(8,128)(2,1)S(1)}, u32[]{:S(2)}, u32[]{:S(2)}) collective-permute-start(bf16[320,256]{1,0:T(8,128)(2,1)S(1)} %get-tuple-element.34), channel_id=1, source_target_pairs={{0,12},{2,14},{4,0},{6,2},{8,4},{10,6},{12,8},{14,10},{1,13},{3,15... | collective-permute-start | bytes 491528 | tf_op jit(solution)/shard_map/ppermute | solution.py:54
  193.1 8.7 %copy-start.3 = (f32[320,1024]{1,0:T(8,128)S(1)}, f32[320,1024]{1,0:T(8,128)}, u32[]{:S(2)}) copy-start(f32[320,1024]{1,0:T(8,128)} %param.12) | copy-start | bytes 3932164
  193.1 8.7 %collective-permute-start.4 = (f32[320,256]{1,0:T(8,128)S(1)}, f32[320,256]{1,0:T(8,128)S(1)}, u32[]{:S(2)}, u32[]{:S(2)}) collective-permute-start(f32[320,256]{1,0:T(8,128)S(1)} %get-tuple-element.3), channel_id=1, source_target_pairs={{0,1},{1,0},{2,3},{3,2},{4,5},{5,4},{6,7},{7,6},{8,9},{9,8},{10,11... | collective-permute-start | bytes 983048 | tf_op jit(solution)/shard_map/ppermute | solution.py:86
  199.9 2.0 collective-permute-start.9
  200.0 2.1 collective-permute-start.14
  200.5 2.1 collective-permute-start.19
  (10 other events, 31.3 us)
Sparse Core Ops, SparseCore 0:
  10.8 68.0 all-gather.1

commit v2 on v1

--- a/solution.py
+++ b/solution.py
@@ -22,15 +22,17 @@
 
 def gather_weight(weight):
     weight_b = weight.astype(jnp.bfloat16)
-    members = lax.axis_size("clients")
-    parts = lax.axis_size("parts")
-    rows = weight.shape[0] // (members * parts)
-    place = lax.axis_index("clients") * parts + lax.axis_index("parts")
-    own = lax.dynamic_slice_in_dim(weight_b, place * rows, rows, 0)
-    return lax.all_gather(own, ("fsdp", "clients", "parts"), axis=0, tiled=True)
+    rows = weight.shape[0] // lax.axis_size("clients")
+    own = lax.dynamic_slice_in_dim(weight_b, lax.axis_index("clients") * rows, rows, 0)
+    width = weight.shape[1] // CHUNKS
+    chunks = []
+    for chunk in range(CHUNKS):
+        piece = own[:, chunk * width : (chunk + 1) * width]
+        chunks.append(lax.all_gather(piece, ("fsdp", "clients"), axis=0, tiled=True))
+    return chunks
 
 
-def scatter_sum(partial):
+def scatter_sum(partial, before):
     n = lax.axis_size("fsdp")
     lines = n // 2
     me = lax.axis_index("fsdp")
@@ -39,46 +41,55 @@
     blocks = partial.reshape(lines, 2, rows, partial.shape[1])
     away = lax.dynamic_index_in_dim(blocks, 1 - side, 1, keepdims=False)
     home = lax.dynamic_index_in_dim(blocks, side, 1, keepdims=False)
-    came = lax.ppermute(
-        away.astype(jnp.bfloat16), "fsdp", [(i, i ^ 1) for i in range(n)]
-    )
+    away = away.astype(jnp.bfloat16)
+    ready = lax.optimization_barrier((away, *before))[0] if before else away
+    came = lax.ppermute(ready, "fsdp", [(i, i ^ 1) for i in range(n)])
     both = home + came.astype(jnp.float32)
     own = lax.dynamic_index_in_dim(both, line, 0, keepdims=False)
     if lines <= 4:
-        total = own
+        total, moved = own, []
         for step in range(1, lines):
             block = lax.dynamic_index_in_dim(
                 both, lax.rem(line + step, lines), 0, keepdims=False
             )
             pairs = [(i, (i + 2 * step) % n) for i in range(n)]
             got = lax.ppermute(block.astype(jnp.bfloat16), "fsdp", pairs)
+            moved.append(got)
             total = total + got.astype(jnp.float32)
-        return total
+        return total, came, away, moved
     groups = [[2 * z + x for z in range(lines)] for x in range(2)]
     got = lax.all_to_all(
         both.astype(jnp.bfloat16), "fsdp", 0, 0, axis_index_groups=groups
     ).astype(jnp.float32)
     others = jnp.arange(lines)[:, None, None] != line
-    return own + jnp.sum(jnp.where(others, got, 0.0), axis=0)
+    return own + jnp.sum(jnp.where(others, got, 0.0), axis=0), came, away, []
 
 
 def per_device(pool_x, pool_cot, assignment, weight, gain, global_variate, client_variate):
     members = lax.axis_size("clients")
     weight_b = gather_weight(weight)
     picked = assignment[0]
-    x_rows = jnp.take(pool_x, picked, axis=0)
-    cot_rows = jnp.take(pool_cot, picked, axis=0)
+    x_rows = pool_x.at[picked].get(mode="promise_in_bounds")
+    cot_rows = pool_cot.at[picked].get(mode="promise_in_bounds")
     width = weight.shape[1] // CHUNKS
     own_variate = client_variate[0]
-    results = []
+    results, came, moved = [], [], []
     for chunk in range(CHUNKS):
         cut = slice(chunk * width, (chunk + 1) * width)
-        keys = jnp.dot(x_rows, weight_b[:, cut], preferred_element_type=jnp.float32)
+        weight_c = weight_b[chunk]
+        if chunk:
+            weight_c = lax.optimization_barrier((weight_c, sent))[0]
+        keys = jnp.dot(x_rows, weight_c, preferred_element_type=jnp.float32)
         dkeys = norm_backward(keys, cot_rows[:, cut], gain)
         partial = lax.dot_general(
             x_rows, dkeys, (((0,), (0,)), ((), ())), preferred_element_type=jnp.float32
         )
-        grads = scatter_sum(partial)
+        before = [came[chunk - 1]] if chunk >= 1 else []
+        if chunk >= 2:
+            before += moved[chunk - 2]
+        grads, arrived, sent, along = scatter_sum(partial, before)
+        came.append(arrived)
+        moved.append(along)
         change = grads - own_variate[:, cut]
         total_change = change
         for step in range(1, members):

time: 214 us -> 269 us (1.26)
  waiting for transfers between devices: 95.5 us -> 140 us
  matrix products: 19.8 us -> 32.2 us
  other arithmetic: 17.5 us -> 10.5 us
  local copies, waits for them, and re-layouts: 37.9 us -> 43.8 us
    all_gather x1 -> x4, waiting for transfers between devices: 26.2 us -> 92.9 us  [gather_weight(): lax.all_gather(piece, ('fsdp', 'clients'), axis=0, tiled=True)]
    ppermute x4, waiting for transfers between devices: 43.8 us -> 19.3 us  [scatter_sum(): came = lax.ppermute(ready, 'fsdp', [(i, i ^ 1) for i in range(n)])]
    dot_general x0 -> x1, local copies, waits for them, and re-layouts: none -> 8.06 us  [per_device(): lax.dot_general(x_rows, dkeys, (((0,), (0,)), ((), ())), preferred_elemen...]
    select_n x1 -> x0, local copies, waits for them, and re-layouts: 7.96 us -> none  [per_device(): x_rows = jnp.take(pool_x, picked, axis=0)]
    select_n x3 -> x1, other arithmetic: 7.81 us -> 0.01 us  [per_device(): x_rows = pool_x.at[picked].get(mode='promise_in_bounds')]
    dot_general x4, matrix products: 7 us -> 14 us  [per_device(): lax.dot_general(x_rows, dkeys, (((0,), (0,)), ((), ())), preferred_elemen...]
    unnamed x26 -> x46, local copies, waits for them, and re-layouts: 1.68 us -> 7.33 us
    dot_general x4, matrix products: 12.8 us -> 18.2 us  [per_device(): keys = jnp.dot(x_rows, weight_c, preferred_element_type=jnp.float32)]
  transfers between devices with their start and end apart: 21 -> 24, of which waited for: 10 -> 13; matrix products, arithmetic and copies ran while one was open for 24% -> 28% of each run, Pallas kernels for 0% -> 0%
where the time goes in v2:
time: 269 us; the launch traced here: 267 us
  waiting for transfers between devices  140 us (52%)
  local copies, waits for them, and re-layouts  43.8 us (16%)
  matrix products  32.2 us (12%)
  starting transfers between devices  26.7 us (10%)
  between operations  14.3 us (5%)
  other arithmetic  10.5 us (4%)
    all_gather x4, waiting for transfers between devices, gather_weight(): lax.all_gather(piece, ('fsdp', 'clients'), axis=0, tiled=True)  92.9 us
    ppermute x12, waiting for transfers between devices, scatter_sum(): got = lax.ppermute(block.astype(jnp.bfloat16), 'fsdp', pairs)  25.6 us
    ppermute x12, starting transfers between devices, scatter_sum(): got = lax.ppermute(block.astype(jnp.bfloat16), 'fsdp', pairs)  22.5 us
    ppermute x4, waiting for transfers between devices, scatter_sum(): came = lax.ppermute(ready, 'fsdp', [(i, i ^ 1) for i in range(n)])  19.3 us
    dot_general x4, matrix products, per_device(): keys = jnp.dot(x_rows, weight_c, preferred_element_type=jnp.float32)  18.2 us
    gather x1, local copies, waits for them, and re-layouts, per_device(): x_rows = pool_x.at[picked].get(mode='promise_in_bounds')  15.8 us
    dot_general x4, matrix products, per_device(): lax.dot_general(x_rows, dkeys, (((0,), (0,)), ((), ())), preferred_elemen...  14 us
    dot_general x1, local copies, waits for them, and re-layouts, per_device(): lax.dot_general(x_rows, dkeys, (((0,), (0,)), ((), ())), preferred_elemen...  8.06 us
  transfers between devices with their start and end apart: 24, of which 13 were waited for; matrix products, arithmetic and copies ran while one was open for 28% of the time, Pallas kernels for 0%

profile of v2, /device:TPU:0, one launch (start us, length us, event | category | flops | bytes accessed | tf_op | source)
XLA Modules:
  0.0 267.1 jit_solution(516543008786836278)
XLA Ops:
  11.3 15.8 %gather_fusion = bf16[1024,2560]{1,0:T(8,128)(2,1)} fusion(bf16[2048,2560]{1,0:T(8,128)(2,1)} %param.7, s32[1024]{0:T(1024)S(1)} %broadcast_clamp_fusion), kind=kCustom, calls=%fused_computation | custom fusion | bytes 10489856 | tf_op jit(solution)/shard_map/gather | solution.py:72
  27.0 7.7 %gather_fusion.1 = bf16[1024,1024]{1,0:T(8,128)(2,1)S(1)} fusion(bf16[2048,1024]{1,0:T(8,128)(2,1)} %param.8, s32[1024]{0:T(1024)S(1)} %broadcast_clamp_fusion), kind=kCustom, calls=%fused_computation.1 | custom fusion | bytes 4198400 | tf_op jit(solution)/shard_map/gather | solution.py:73
  37.2 8.1 %copy.25 = bf16[2560,1024]{1,0:T(8,128)(2,1)} copy(bf16[2560,1024]{0,1:T(8,128)(2,1)} %bitcast.222) | data formatting | bytes 10485760 | tf_op jit(solution)/shard_map/dot_general | solution.py:84
  45.9 6.5 %all-gather.5.cloned.1.call-done = bf16[2560,256]{1,0:T(8,128)(2,1)} async-done(((bf16[160,256]{1,0:T(8,128)(2,1)}), bf16[2560,256]{1,0:T(8,128)(2,1)}) %all-gather.5.cloned.1.call-update) | async-done | bytes 1310736 | tf_op jit(solution)/shard_map/all_gather | solution.py:31
  52.4 4.5 %multiply_reduce_fusion.7 = (f32[1024,2]{0,1:T(2,128)S(1)}, f32[1024,256]{0,1:T(8,128)S(1)}) fusion(bf16[1024,2560]{1,0:T(8,128)(2,1)} %gather_fusion, bf16[2560,256]{1,0:T(8,128)(2,1)} %all-gather.5.cloned.1.call-done), kind=kOutput, calls=%fused_computation.60 | convolution fusion | flops 1342699520 | bytes 7610368 | tf_op jit(solution)/shard_map/dot_general | solution.py:82
  57.6 4.1 %fusion.34 = f32[4,2,320,256]{3,2,1,0:T(8,128)S(1)} fusion(bf16[4,2,320,1024]{3,2,1,0:T(8,128)(2,1)} %bitcast.223, bf16[1024,256]{0,1:T(8,128)(2,1)S(1)} %fusion.5), kind=kOutput, calls=%fused_computation.76 | convolution fusion | flops 1342177280 | bytes 8388608 | tf_op jit(solution)/shard_map/dot_general | solution.py:84
  64.0 28.4 %all-gather.7.cloned.1.call-done = bf16[2560,256]{1,0:T(8,128)(2,1)} async-done(((bf16[160,256]{1,0:T(8,128)(2,1)}), bf16[2560,256]{1,0:T(8,128)(2,1)}) %all-gather.7.cloned.1.call-update) | async-done | bytes 1310736 | tf_op jit(solution)/shard_map/all_gather | solution.py:31
  92.4 4.5 %multiply_reduce_fusion.5 = (f32[1024,2]{0,1:T(2,128)S(1)}, f32[1024,256]{0,1:T(8,128)S(1)}) fusion(bf16[1024,2560]{1,0:T(8,128)(2,1)} %gather_fusion, bf16[2560,256]{1,0:T(8,128)(2,1)} %all-gather.7.cloned.1.call-done), kind=kOutput, calls=%fused_computation.57 | convolution fusion | flops 1342699520 | bytes 7610368 | tf_op jit(solution)/shard_map/dot_general | solution.py:82
  97.6 4.1 %fusion.32 = f32[4,2,320,256]{3,2,1,0:T(8,128)S(1)} fusion(bf16[4,2,320,1024]{3,2,1,0:T(8,128)(2,1)} %bitcast.224, bf16[1024,256]{0,1:T(8,128)(2,1)S(1)} %fusion.8), kind=kOutput, calls=%fused_computation.74 | convolution fusion | flops 1342177280 | bytes 8388608 | tf_op jit(solution)/shard_map/dot_general | solution.py:84
  103.2 29.0 %all-gather.9.cloned.1.call-done = bf16[2560,256]{1,0:T(8,128)(2,1)} async-done(((bf16[160,256]{1,0:T(8,128)(2,1)}), bf16[2560,256]{1,0:T(8,128)(2,1)}) %all-gather.9.cloned.1.call-update) | async-done | bytes 1310736 | tf_op jit(solution)/shard_map/all_gather | solution.py:31
  132.3 4.5 %multiply_reduce_fusion.3 = (f32[1024,2]{0,1:T(2,128)S(1)}, f32[1024,256]{0,1:T(8,128)S(1)}) fusion(bf16[1024,2560]{1,0:T(8,128)(2,1)} %gather_fusion, bf16[2560,256]{1,0:T(8,128)(2,1)} %all-gather.9.cloned.1.call-done), kind=kOutput, calls=%fused_computation.54 | convolution fusion | flops 1342699520 | bytes 7610368 | tf_op jit(solution)/shard_map/dot_general | solution.py:82
  137.4 4.1 %fusion.30 = f32[4,2,320,256]{3,2,1,0:T(8,128)S(1)} fusion(bf16[4,2,320,1024]{3,2,1,0:T(8,128)(2,1)} %bitcast.225, bf16[1024,256]{0,1:T(8,128)(2,1)S(1)} %fusion.11), kind=kOutput, calls=%fused_computation.72 | convolution fusion | flops 1342177280 | bytes 8388608 | tf_op jit(solution)/shard_map/dot_general | solution.py:84
  143.1 28.9 %all-gather.11.cloned.1.call-done = bf16[2560,256]{1,0:T(8,128)(2,1)} async-done(((bf16[160,256]{1,0:T(8,128)(2,1)}), bf16[2560,256]{1,0:T(8,128)(2,1)}) %all-gather.11.cloned.1.call-update) | async-done | bytes 1310736 | tf_op jit(solution)/shard_map/all_gather | solution.py:31
  172.6 4.8 %multiply_reduce_fusion.1 = (f32[1024,2]{0,1:T(2,128)S(1)}, f32[1024,256]{0,1:T(8,128)S(1)}) fusion(bf16[1024,2560]{1,0:T(8,128)(2,1)} %gather_fusion, bf16[2560,256]{1,0:T(8,128)(2,1)} %all-gather.11.cloned.1.call-done), kind=kOutput, calls=%fused_computation.51 | convolution fusion | flops 1342699520 | bytes 7610368 | tf_op jit(solution)/shard_map/dot_general | solution.py:82
  177.8 11.1 %collective-permute-done.5 = bf16[4,320,256]{2,1,0:T(8,128)(2,1)S(1)} collective-permute-done((bf16[4,320,256]{2,1,0:T(8,128)(2,1)S(1)}, bf16[4,320,256]{2,1,0:T(8,128)(2,1)S(1)}, u32[]{:S(2)}, u32[]{:S(2)}) %collective-permute-start.5) | collective-permute-done | bytes 655392 | tf_op jit(solution)/shard_map/ppermute | solution.py:46
  193.7 4.8 %collective-permute-done.1 = bf16[320,256]{1,0:T(8,128)(2,1)S(1)} collective-permute-done((bf16[320,256]{1,0:T(8,128)(2,1)S(1)}, bf16[320,256]{1,0:T(8,128)(2,1)S(1)}, u32[]{:S(2)}, u32[]{:S(2)}) %collective-permute-start.1) | collective-permute-done | bytes 163872 | tf_op jit(solution)/shard_map/ppermute | solution.py:56
  198.5 5.5 %collective-permute-done.2 = bf16[320,256]{1,0:T(8,128)(2,1)S(1)} collective-permute-done((bf16[320,256]{1,0:T(8,128)(2,1)S(1)}, bf16[320,256]{1,0:T(8,128)(2,1)S(1)}, u32[]{:S(2)}, u32[]{:S(2)}) %collective-permute-start.2) | collective-permute-done | bytes 163872 | tf_op jit(solution)/shard_map/ppermute | solution.py:56
  204.7 3.5 %collective-permute-start.6 = (bf16[320,256]{1,0:T(8,128)(2,1)S(1)}, bf16[320,256]{1,0:T(8,128)(2,1)S(1)}, u32[]{:S(2)}, u32[]{:S(2)}) collective-permute-start(bf16[320,256]{1,0:T(8,128)(2,1)S(1)} %get-tuple-element.46), channel_id=1, source_target_pairs={{0,4},{2,6},{4,8},{6,10},{8,12},{10,14},{12,0},{14,2},{1,5},{3,7},... | collective-permute-start | bytes 491528 | tf_op jit(solution)/shard_map/ppermute | solution.py:56
  213.4 5.6 %collective-permute-done.7 = bf16[320,256]{1,0:T(8,128)(2,1)S(1)} collective-permute-done((bf16[320,256]{1,0:T(8,128)(2,1)S(1)}, bf16[320,256]{1,0:T(8,128)(2,1)S(1)}, u32[]{:S(2)}, u32[]{:S(2)}) %collective-permute-start.7) | collective-permute-done | bytes 163872 | tf_op jit(solution)/shard_map/ppermute | solution.py:56
  221.5 3.9 %collective-permute-start.11 = (bf16[320,256]{1,0:T(8,128)(2,1)S(1)}, bf16[320,256]{1,0:T(8,128)(2,1)S(1)}, u32[]{:S(2)}, u32[]{:S(2)}) collective-permute-start(bf16[320,256]{1,0:T(8,128)(2,1)S(1)} %get-tuple-element.38), channel_id=1, source_target_pairs={{0,4},{2,6},{4,8},{6,10},{8,12},{10,14},{12,0},{14,2},{1,5},{3,7},... | collective-permute-start | bytes 491528 | tf_op jit(solution)/shard_map/ppermute | solution.py:56
  227.8 7.8 %collective-permute-done.15 = bf16[4,320,256]{2,1,0:T(8,128)(2,1)S(1)} collective-permute-done((bf16[4,320,256]{2,1,0:T(8,128)(2,1)S(1)}, bf16[4,320,256]{2,1,0:T(8,128)(2,1)S(1)}, u32[]{:S(2)}, u32[]{:S(2)}) %collective-permute-start.15) | collective-permute-done | bytes 655392 | tf_op jit(solution)/shard_map/ppermute | solution.py:46
  236.6 4.0 %collective-permute-start.16 = (bf16[320,256]{1,0:T(8,128)(2,1)}, bf16[320,256]{1,0:T(8,128)(2,1)}, u32[]{:S(2)}, u32[]{:S(2)}) collective-permute-start(bf16[320,256]{1,0:T(8,128)(2,1)} %get-tuple-element.41), channel_id=1, source_target_pairs={{0,4},{2,6},{4,8},{6,10},{8,12},{10,14},{12,0},{14,2},{1,5},{3,7},... | collective-permute-start | bytes 491528 | tf_op jit(solution)/shard_map/ppermute | solution.py:56
  242.9 3.4 %collective-permute-done.16 = bf16[320,256]{1,0:T(8,128)(2,1)} collective-permute-done((bf16[320,256]{1,0:T(8,128)(2,1)}, bf16[320,256]{1,0:T(8,128)(2,1)}, u32[]{:S(2)}, u32[]{:S(2)}) %collective-permute-start.16) | collective-permute-done | bytes 163872 | tf_op jit(solution)/shard_map/ppermute | solution.py:56
  246.3 5.2 %collective-permute-done.17 = bf16[320,256]{1,0:T(8,128)(2,1)} collective-permute-done((bf16[320,256]{1,0:T(8,128)(2,1)}, bf16[320,256]{1,0:T(8,128)(2,1)}, u32[]{:S(2)}, u32[]{:S(2)}) %collective-permute-start.17) | collective-permute-done | bytes 163872 | tf_op jit(solution)/shard_map/ppermute | solution.py:56
  (122 shorter events, 43.0 us)
Async XLA Ops:
  7.2 45.2 %all-gather.5.cloned.1.call-start = ((), (), s32[]{:S(2)}) async-start(), calls=%async_computation | async-start | bytes 1392640 | tf_op jit(solution)/shard_map/all_gather | solution.py:31
  9.1 83.3 %all-gather.7.cloned.1.call-start = ((), (), s32[]{:S(2)}) async-start(), calls=%async_computation.1 | async-start | bytes 1392640 | tf_op jit(solution)/shard_map/all_gather | solution.py:31
  9.9 122.4 %all-gather.9.cloned.1.call-start = ((), (), s32[]{:S(2)}) async-start(), calls=%async_computation.2 | async-start | bytes 1392640 | tf_op jit(solution)/shard_map/all_gather | solution.py:31
  10.6 161.5 %all-gather.11.cloned.1.call-start = ((), (), s32[]{:S(2)}) async-start(), calls=%async_computation.3 | async-start | bytes 1392640 | tf_op jit(solution)/shard_map/all_gather | solution.py:31
  63.4 108.7 %collective-permute-start = (bf16[4,320,256]{2,1,0:T(8,128)(2,1)S(1)}, bf16[4,320,256]{2,1,0:T(8,128)(2,1)S(1)}, u32[]{:S(2)}, u32[]{:S(2)}) collective-permute-start(bf16[4,320,256]{2,1,0:T(8,128)(2,1)S(1)} %fusion.24), channel_id=1, source_target_pairs={{0,2},{2,0},{4,6},{6,4},{8,10},{10,8},{12,14},{14,12},{1,3},{3,1},... | collective-permute-start | bytes 1966088 | tf_op jit(solution)/shard_map/ppermute | solution.py:46
  172.1 16.9 %collective-permute-start.5 = (bf16[4,320,256]{2,1,0:T(8,128)(2,1)S(1)}, bf16[4,320,256]{2,1,0:T(8,128)(2,1)S(1)}, u32[]{:S(2)}, u32[]{:S(2)}) collective-permute-start(bf16[4,320,256]{2,1,0:T(8,128)(2,1)S(1)} %fusion.25), channel_id=1, source_target_pairs={{0,2},{2,0},{4,6},{6,4},{8,10},{10,8},{12,14},{14,12},{1,3},{3,1},... | collective-permute-start | bytes 1966088 | tf_op jit(solution)/shard_map/ppermute | solution.py:46
  189.4 9.1 %collective-permute-start.1 = (bf16[320,256]{1,0:T(8,128)(2,1)S(1)}, bf16[320,256]{1,0:T(8,128)(2,1)S(1)}, u32[]{:S(2)}, u32[]{:S(2)}) collective-permute-start(bf16[320,256]{1,0:T(8,128)(2,1)S(1)} %get-tuple-element.49), channel_id=1, source_target_pairs={{0,4},{2,6},{4,8},{6,10},{8,12},{10,14},{12,0},{14,2},{1,5},{3,7},... | collective-permute-start | bytes 491528 | tf_op jit(solution)/shard_map/ppermute | solution.py:56
  190.0 14.0 %collective-permute-start.2 = (bf16[320,256]{1,0:T(8,128)(2,1)S(1)}, bf16[320,256]{1,0:T(8,128)(2,1)S(1)}, u32[]{:S(2)}, u32[]{:S(2)}) collective-permute-start(bf16[320,256]{1,0:T(8,128)(2,1)S(1)} %get-tuple-element.48), channel_id=1, source_target_pairs={{0,8},{2,10},{4,12},{6,14},{8,0},{10,2},{12,4},{14,6},{1,9},{3,11}... | collective-permute-start | bytes 491528 | tf_op jit(solution)/shard_map/ppermute | solution.py:56
  192.2 11.8 %collective-permute-start.3 = (bf16[320,256]{1,0:T(8,128)(2,1)S(1)}, bf16[320,256]{1,0:T(8,128)(2,1)S(1)}, u32[]{:S(2)}, u32[]{:S(2)}) collective-permute-start(bf16[320,256]{1,0:T(8,128)(2,1)S(1)} %get-tuple-element.47), channel_id=1, source_target_pairs={{0,12},{2,14},{4,0},{6,2},{8,4},{10,6},{12,8},{14,10},{1,13},{3,15... | collective-permute-start | bytes 491528 | tf_op jit(solution)/shard_map/ppermute | solution.py:56
  204.0 15.2 %collective-permute-start.10 = (bf16[4,320,256]{2,1,0:T(8,128)(2,1)S(1)}, bf16[4,320,256]{2,1,0:T(8,128)(2,1)S(1)}, u32[]{:S(2)}, u32[]{:S(2)}) collective-permute-start(bf16[4,320,256]{2,1,0:T(8,128)(2,1)S(1)} %fusion.26), channel_id=1, source_target_pairs={{0,2},{2,0},{4,6},{6,4},{8,10},{10,8},{12,14},{14,12},{1,3},{3,1},... | collective-permute-start | bytes 1966088 | tf_op jit(solution)/shard_map/ppermute | solution.py:46
  204.7 8.7 %collective-permute-start.6 = (bf16[320,256]{1,0:T(8,128)(2,1)S(1)}, bf16[320,256]{1,0:T(8,128)(2,1)S(1)}, u32[]{:S(2)}, u32[]{:S(2)}) collective-permute-start(bf16[320,256]{1,0:T(8,128)(2,1)S(1)} %get-tuple-element.46), channel_id=1, source_target_pairs={{0,4},{2,6},{4,8},{6,10},{8,12},{10,14},{12,0},{14,2},{1,5},{3,7},... | collective-permute-start | bytes 491528 | tf_op jit(solution)/shard_map/ppermute | solution.py:56
  208.2 10.8 %collective-permute-start.7 = (bf16[320,256]{1,0:T(8,128)(2,1)S(1)}, bf16[320,256]{1,0:T(8,128)(2,1)S(1)}, u32[]{:S(2)}, u32[]{:S(2)}) collective-permute-start(bf16[320,256]{1,0:T(8,128)(2,1)S(1)} %get-tuple-element.45), channel_id=1, source_target_pairs={{0,8},{2,10},{4,12},{6,14},{8,0},{10,2},{12,4},{14,6},{1,9},{3,11}... | collective-permute-start | bytes 491528 | tf_op jit(solution)/shard_map/ppermute | solution.py:56
  208.8 10.2 %collective-permute-start.8 = (bf16[320,256]{1,0:T(8,128)(2,1)S(1)}, bf16[320,256]{1,0:T(8,128)(2,1)S(1)}, u32[]{:S(2)}, u32[]{:S(2)}) collective-permute-start(bf16[320,256]{1,0:T(8,128)(2,1)S(1)} %get-tuple-element.44), channel_id=1, source_target_pairs={{0,12},{2,14},{4,0},{6,2},{8,4},{10,6},{12,8},{14,10},{1,13},{3,15... | collective-permute-start | bytes 491528 | tf_op jit(solution)/shard_map/ppermute | solution.py:56
  219.2 16.3 %collective-permute-start.15 = (bf16[4,320,256]{2,1,0:T(8,128)(2,1)S(1)}, bf16[4,320,256]{2,1,0:T(8,128)(2,1)S(1)}, u32[]{:S(2)}, u32[]{:S(2)}) collective-permute-start(bf16[4,320,256]{2,1,0:T(8,128)(2,1)S(1)} %fusion.27), channel_id=1, source_target_pairs={{0,2},{2,0},{4,6},{6,4},{8,10},{10,8},{12,14},{14,12},{1,3},{3,1},... | collective-permute-start | bytes 1966088 | tf_op jit(solution)/shard_map/ppermute | solution.py:46
  221.5 20.0 %collective-permute-start.11 = (bf16[320,256]{1,0:T(8,128)(2,1)S(1)}, bf16[320,256]{1,0:T(8,128)(2,1)S(1)}, u32[]{:S(2)}, u32[]{:S(2)}) collective-permute-start(bf16[320,256]{1,0:T(8,128)(2,1)S(1)} %get-tuple-element.38), channel_id=1, source_target_pairs={{0,4},{2,6},{4,8},{6,10},{8,12},{10,14},{12,0},{14,2},{1,5},{3,7},... | collective-permute-start | bytes 491528 | tf_op jit(solution)/shard_map/ppermute | solution.py:56
  225.4 17.6 %collective-permute-start.12 = (bf16[320,256]{1,0:T(8,128)(2,1)}, bf16[320,256]{1,0:T(8,128)(2,1)S(1)}, u32[]{:S(2)}, u32[]{:S(2)}) collective-permute-start(bf16[320,256]{1,0:T(8,128)(2,1)} %get-tuple-element.40), channel_id=1, source_target_pairs={{0,8},{2,10},{4,12},{6,14},{8,0},{10,2},{12,4},{14,6},{1,9},{3,11}... | collective-permute-start | bytes 491528 | tf_op jit(solution)/shard_map/ppermute | solution.py:56
  227.4 15.5 %collective-permute-start.13 = (bf16[320,256]{1,0:T(8,128)(2,1)}, bf16[320,256]{1,0:T(8,128)(2,1)}, u32[]{:S(2)}, u32[]{:S(2)}) collective-permute-start(bf16[320,256]{1,0:T(8,128)(2,1)} %get-tuple-element.39), channel_id=1, source_target_pairs={{0,12},{2,14},{4,0},{6,2},{8,4},{10,6},{12,8},{14,10},{1,13},{3,15... | collective-permute-start | bytes 491528 | tf_op jit(solution)/shard_map/ppermute | solution.py:56
  236.6 9.8 %collective-permute-start.16 = (bf16[320,256]{1,0:T(8,128)(2,1)}, bf16[320,256]{1,0:T(8,128)(2,1)}, u32[]{:S(2)}, u32[]{:S(2)}) collective-permute-start(bf16[320,256]{1,0:T(8,128)(2,1)} %get-tuple-element.41), channel_id=1, source_target_pairs={{0,4},{2,6},{4,8},{6,10},{8,12},{10,14},{12,0},{14,2},{1,5},{3,7},... | collective-permute-start | bytes 491528 | tf_op jit(solution)/shard_map/ppermute | solution.py:56
  240.6 10.9 %collective-permute-start.17 = (bf16[320,256]{1,0:T(8,128)(2,1)}, bf16[320,256]{1,0:T(8,128)(2,1)}, u32[]{:S(2)}, u32[]{:S(2)}) collective-permute-start(bf16[320,256]{1,0:T(8,128)(2,1)} %get-tuple-element.43), channel_id=1, source_target_pairs={{0,8},{2,10},{4,12},{6,14},{8,0},{10,2},{12,4},{14,6},{1,9},{3,11}... | collective-permute-start | bytes 491528 | tf_op jit(solution)/shard_map/ppermute | solution.py:56
  241.5 10.0 %collective-permute-start.18 = (bf16[320,256]{1,0:T(8,128)(2,1)}, bf16[320,256]{1,0:T(8,128)(2,1)}, u32[]{:S(2)}, u32[]{:S(2)}) collective-permute-start(bf16[320,256]{1,0:T(8,128)(2,1)} %get-tuple-element.42), channel_id=1, source_target_pairs={{0,12},{2,14},{4,0},{6,2},{8,4},{10,6},{12,8},{14,10},{1,13},{3,15... | collective-permute-start | bytes 491528 | tf_op jit(solution)/shard_map/ppermute | solution.py:56
  253.3 3.6 %collective-permute-start.4 = (f32[320,256]{1,0:T(8,128)S(1)}, f32[320,256]{1,0:T(8,128)S(1)}, u32[]{:S(2)}, u32[]{:S(2)}) collective-permute-start(f32[320,256]{1,0:T(8,128)S(1)} %get-tuple-element.15), channel_id=1, source_target_pairs={{0,1},{1,0},{2,3},{3,2},{4,5},{5,4},{6,7},{7,6},{8,9},{9,8},{10,11... | collective-permute-start | bytes 983048 | tf_op jit(solution)/shard_map/ppermute | solution.py:97
  254.6 2.9 %collective-permute-start.9 = (f32[320,256]{1,0:T(8,128)S(1)}, f32[320,256]{1,0:T(8,128)S(1)}, u32[]{:S(2)}, u32[]{:S(2)}) collective-permute-start(f32[320,256]{1,0:T(8,128)S(1)} %get-tuple-element.17), channel_id=1, source_target_pairs={{0,1},{1,0},{2,3},{3,2},{4,5},{5,4},{6,7},{7,6},{8,9},{9,8},{10,11... | collective-permute-start | bytes 983048 | tf_op jit(solution)/shard_map/ppermute | solution.py:97
  255.1 2.4 collective-permute-start.14
  255.2 2.3 collective-permute-start.19
  (21 other events, 167.6 us)
Sparse Core Ops, SparseCore 0:
  10.9 41.4 all-gather.4
  54.7 37.6 all-gather.6
  94.7 37.5 all-gather.8
  134.4 37.6 all-gather.10

commit v3 on v2

--- a/solution.py
+++ b/solution.py
@@ -24,12 +24,7 @@
     weight_b = weight.astype(jnp.bfloat16)
     rows = weight.shape[0] // lax.axis_size("clients")
     own = lax.dynamic_slice_in_dim(weight_b, lax.axis_index("clients") * rows, rows, 0)
-    width = weight.shape[1] // CHUNKS
-    chunks = []
-    for chunk in range(CHUNKS):
-        piece = own[:, chunk * width : (chunk + 1) * width]
-        chunks.append(lax.all_gather(piece, ("fsdp", "clients"), axis=0, tiled=True))
-    return chunks
+    return lax.all_gather(own, ("fsdp", "clients"), axis=0, tiled=True)
 
 
 def scatter_sum(partial, before):
@@ -45,24 +40,25 @@
     ready = lax.optimization_barrier((away, *before))[0] if before else away
     came = lax.ppermute(ready, "fsdp", [(i, i ^ 1) for i in range(n)])
     both = home + came.astype(jnp.float32)
+    narrow = both.astype(jnp.bfloat16)
     own = lax.dynamic_index_in_dim(both, line, 0, keepdims=False)
     if lines <= 4:
         total, moved = own, []
         for step in range(1, lines):
             block = lax.dynamic_index_in_dim(
-                both, lax.rem(line + step, lines), 0, keepdims=False
+                narrow, lax.rem(line + step, lines), 0, keepdims=False
             )
             pairs = [(i, (i + 2 * step) % n) for i in range(n)]
-            got = lax.ppermute(block.astype(jnp.bfloat16), "fsdp", pairs)
+            got = lax.ppermute(block, "fsdp", pairs)
             moved.append(got)
             total = total + got.astype(jnp.float32)
-        return total, came, away, moved
+        return total, narrow, away, moved
     groups = [[2 * z + x for z in range(lines)] for x in range(2)]
     got = lax.all_to_all(
-        both.astype(jnp.bfloat16), "fsdp", 0, 0, axis_index_groups=groups
+        narrow, "fsdp", 0, 0, axis_index_groups=groups
     ).astype(jnp.float32)
     others = jnp.arange(lines)[:, None, None] != line
-    return own + jnp.sum(jnp.where(others, got, 0.0), axis=0), came, away, []
+    return own + jnp.sum(jnp.where(others, got, 0.0), axis=0), narrow, away, []
 
 
 def per_device(pool_x, pool_cot, assignment, weight, gain, global_variate, client_variate):
@@ -76,10 +72,9 @@
     results, came, moved = [], [], []
     for chunk in range(CHUNKS):
         cut = slice(chunk * width, (chunk + 1) * width)
-        weight_c = weight_b[chunk]
         if chunk:
-            weight_c = lax.optimization_barrier((weight_c, sent))[0]
-        keys = jnp.dot(x_rows, weight_c, preferred_element_type=jnp.float32)
+            weight_b = lax.optimization_barrier((weight_b, sent))[0]
+        keys = jnp.dot(x_rows, weight_b[:, cut], preferred_element_type=jnp.float32)
         dkeys = norm_backward(keys, cot_rows[:, cut], gain)
         partial = lax.dot_general(
             x_rows, dkeys, (((0,), (0,)), ((), ())), preferred_element_type=jnp.float32

time: 269 us -> 186 us (0.69)
  waiting for transfers between devices: 140 us -> 79.6 us
  matrix products: 32.2 us -> 15.8 us
  starting transfers between devices: 26.7 us -> 20.1 us
    all_gather x4 -> x1, waiting for transfers between devices: 92.9 us -> 24.1 us  [gather_weight(): return lax.all_gather(own, ('fsdp', 'clients'), axis=0, tiled=True)]
    ppermute x4, waiting for transfers between devices: 19.3 us -> 34.4 us  [scatter_sum(): came = lax.ppermute(ready, 'fsdp', [(i, i ^ 1) for i in range(n)])]
    dot_general x4, matrix products: 18.2 us -> 9.46 us  [per_device(): keys = jnp.dot(x_rows, weight_b[:, cut], preferred_element_type=jnp.float32)]
    dot_general x4, matrix products: 14 us -> 6.33 us  [per_device(): lax.dot_general(x_rows, dkeys, (((0,), (0,)), ((), ())), preferred_elemen...]
    ppermute x12, starting transfers between devices: 22.5 us -> 15.5 us  [scatter_sum(): got = lax.ppermute(block, 'fsdp', pairs)]
    ppermute x12, waiting for transfers between devices: 25.6 us -> 20.7 us  [scatter_sum(): got = lax.ppermute(block, 'fsdp', pairs)]
    convert_element_type x0 -> x4, other arithmetic: none -> 2.88 us  [scatter_sum(): narrow = both.astype(jnp.bfloat16)]
    unnamed x46 -> x30, local copies, waits for them, and re-layouts: 7.33 us -> 5.74 us
  transfers between devices with their start and end apart: 24 -> 21, of which waited for: 13 -> 10; matrix products, arithmetic and copies ran while one was open for 28% -> 30% of each run, Pallas kernels for 0% -> 0%
where the time goes in v3:
time: 186 us; the launch traced here: 185 us
  waiting for transfers between devices  79.6 us (43%)
  local copies, waits for them, and re-layouts  42.2 us (23%)
  starting transfers between devices  20.1 us (11%)
  matrix products  15.8 us (8%)
  between operations  14.5 us (8%)
  other arithmetic  12.9 us (7%)
    ppermute x4, waiting for transfers between devices, scatter_sum(): came = lax.ppermute(ready, 'fsdp', [(i, i ^ 1) for i in range(n)])  34.4 us
    all_gather x1, waiting for transfers between devices, gather_weight(): return lax.all_gather(own, ('fsdp', 'clients'), axis=0, tiled=True)  24.1 us
    ppermute x12, waiting for transfers between devices, scatter_sum(): got = lax.ppermute(block, 'fsdp', pairs)  20.7 us
    gather x1, local copies, waits for them, and re-layouts, per_device(): x_rows = pool_x.at[picked].get(mode='promise_in_bounds')  15.9 us
    ppermute x12, starting transfers between devices, scatter_sum(): got = lax.ppermute(block, 'fsdp', pairs)  15.5 us
    dot_general x4, matrix products, per_device(): keys = jnp.dot(x_rows, weight_b[:, cut], preferred_element_type=jnp.float32)  9.46 us
    dot_general x1, local copies, waits for them, and re-layouts, per_device(): lax.dot_general(x_rows, dkeys, (((0,), (0,)), ((), ())), preferred_elemen...  8 us
    gather x1, local copies, waits for them, and re-layouts, per_device(): cot_rows = pool_cot.at[picked].get(mode='promise_in_bounds')  7.71 us
  transfers between devices with their start and end apart: 21, of which 10 were waited for; matrix products, arithmetic and copies ran while one was open for 30% of the time, Pallas kernels for 0%

profile of v3, /device:TPU:0, one launch (start us, length us, event | category | flops | bytes accessed | tf_op | source)
XLA Modules:
  0.0 185.0 jit_solution(10598343800277661922)
XLA Ops:
  7.2 1.9 %dynamic-slice_convert_fusion.4 = bf16[160,1024]{1,0:T(8,128)(2,1)} fusion(f32[320,1024]{1,0:T(8,128)} %param.10, s32[]{:T(128)S(6)} %select_n.62), kind=kLoop, calls=%fused_computation.77 | loop fusion | bytes 655364 | tf_op jit(solution)/shard_map/convert_element_type | solution.py:24
  9.9 7.7 %gather_fusion.1 = bf16[1024,1024]{1,0:T(8,128)(2,1)S(1)} fusion(bf16[2048,1024]{1,0:T(8,128)(2,1)} %param.8, s32[1024]{0:T(1024)S(1)} %broadcast_clamp_fusion), kind=kCustom, calls=%fused_computation.1 | custom fusion | bytes 4198400 | tf_op jit(solution)/shard_map/gather | solution.py:69
  21.6 15.9 %gather_fusion = bf16[1024,2560]{1,0:T(8,128)(2,1)} fusion(bf16[2048,2560]{1,0:T(8,128)(2,1)} %param.7, s32[1024]{0:T(1024)S(1)} %broadcast_clamp_fusion), kind=kCustom, calls=%fused_computation | custom fusion | bytes 10489856 | tf_op jit(solution)/shard_map/gather | solution.py:68
  37.5 8.0 %copy.22 = bf16[2560,1024]{1,0:T(8,128)(2,1)} copy(bf16[2560,1024]{0,1:T(8,128)(2,1)} %bitcast.210) | data formatting | bytes 10485760 | tf_op jit(solution)/shard_map/dot_general | solution.py:79
  45.5 24.1 %all-gather.2.cloned.1.call-done = bf16[2560,1024]{1,0:T(8,128)(2,1)} async-done(((bf16[160,1024]{1,0:T(8,128)(2,1)}), bf16[2560,1024]{1,0:T(8,128)(2,1)}) %all-gather.2.cloned.1.call-update) | async-done | bytes 5242896 | tf_op jit(solution)/shard_map/all_gather | solution.py:27
  69.6 4.4 %multiply_reduce_fusion.7 = (f32[1024,2]{0,1:T(2,128)S(1)}, f32[1024,256]{0,1:T(8,128)S(1)}) fusion(bf16[1024,2560]{1,0:T(8,128)(2,1)} %gather_fusion, bf16[2560,1024]{1,0:T(8,128)(2,1)} %all-gather.2.cloned.1.call-done), kind=kOutput, calls=%fused_computation.68 | convolution fusion | flops 1342699520 | bytes 7610368 | tf_op jit(solution)/shard_map/dot_general | solution.py:77
  74.8 1.8 copy-done
  87.7 7.4 %collective-permute-done = bf16[4,320,256]{2,1,0:T(8,128)(2,1)S(1)} collective-permute-done((bf16[4,320,256]{2,1,0:T(8,128)(2,1)S(1)}, bf16[4,320,256]{2,1,0:T(8,128)(2,1)S(1)}, u32[]{:S(2)}, u32[]{:S(2)}) %collective-permute-start) | collective-permute-done | bytes 655392 | tf_op jit(solution)/shard_map/ppermute | solution.py:41
  96.0 1.8 multiply_reduce_fusion.1
  98.6 2.0 %collective-permute-start.3 = (bf16[320,256]{1,0:T(8,128)(2,1)S(1)}, bf16[320,256]{1,0:T(8,128)(2,1)S(1)}, u32[]{:S(2)}, u32[]{:S(2)}) collective-permute-start(bf16[320,256]{1,0:T(8,128)(2,1)S(1)} %get-tuple-element.55), channel_id=1, source_target_pairs={{0,12},{2,14},{4,0},{6,2},{8,4},{10,6},{12,8},{14,10},{1,13},{3,15... | collective-permute-start | bytes 491528 | tf_op jit(solution)/shard_map/ppermute | solution.py:52
  102.6 8.9 %collective-permute-done.5 = bf16[4,320,256]{2,1,0:T(8,128)(2,1)S(1)} collective-permute-done((bf16[4,320,256]{2,1,0:T(8,128)(2,1)S(1)}, bf16[4,320,256]{2,1,0:T(8,128)(2,1)S(1)}, u32[]{:S(2)}, u32[]{:S(2)}) %collective-permute-start.5) | collective-permute-done | bytes 655392 | tf_op jit(solution)/shard_map/ppermute | solution.py:41
  112.8 2.6 %collective-permute-done.2 = bf16[320,256]{1,0:T(8,128)(2,1)S(1)} collective-permute-done((bf16[320,256]{1,0:T(8,128)(2,1)S(1)}, bf16[320,256]{1,0:T(8,128)(2,1)S(1)}, u32[]{:S(2)}, u32[]{:S(2)}) %collective-permute-start.2) | collective-permute-done | bytes 163872 | tf_op jit(solution)/shard_map/ppermute | solution.py:52
  116.9 1.7 fusion.36
  118.7 1.9 %collective-permute-start.7 = (bf16[320,256]{1,0:T(8,128)(2,1)S(1)}, bf16[320,256]{1,0:T(8,128)(2,1)S(1)}, u32[]{:S(2)}, u32[]{:S(2)}) collective-permute-start(bf16[320,256]{1,0:T(8,128)(2,1)S(1)} %get-tuple-element.53), channel_id=1, source_target_pairs={{0,8},{2,10},{4,12},{6,14},{8,0},{10,2},{12,4},{14,6},{1,9},{3,11}... | collective-permute-start | bytes 491528 | tf_op jit(solution)/shard_map/ppermute | solution.py:52
  120.6 1.9 %collective-permute-start.6 = (bf16[320,256]{1,0:T(8,128)(2,1)S(1)}, bf16[320,256]{1,0:T(8,128)(2,1)S(1)}, u32[]{:S(2)}, u32[]{:S(2)}) collective-permute-start(bf16[320,256]{1,0:T(8,128)(2,1)S(1)} %get-tuple-element.54), channel_id=1, source_target_pairs={{0,4},{2,6},{4,8},{6,10},{8,12},{10,14},{12,0},{14,2},{1,5},{3,7},... | collective-permute-start | bytes 491528 | tf_op jit(solution)/shard_map/ppermute | solution.py:52
  122.6 7.4 %collective-permute-done.10 = bf16[4,320,256]{2,1,0:T(8,128)(2,1)S(1)} collective-permute-done((bf16[4,320,256]{2,1,0:T(8,128)(2,1)S(1)}, bf16[4,320,256]{2,1,0:T(8,128)(2,1)S(1)}, u32[]{:S(2)}, u32[]{:S(2)}) %collective-permute-start.10) | collective-permute-done | bytes 655392 | tf_op jit(solution)/shard_map/ppermute | solution.py:41
  130.2 5.0 %collective-permute-done.7 = bf16[320,256]{1,0:T(8,128)(2,1)S(1)} collective-permute-done((bf16[320,256]{1,0:T(8,128)(2,1)S(1)}, bf16[320,256]{1,0:T(8,128)(2,1)S(1)}, u32[]{:S(2)}, u32[]{:S(2)}) %collective-permute-start.7) | collective-permute-done | bytes 163872 | tf_op jit(solution)/shard_map/ppermute | solution.py:52
  136.6 3.8 %collective-permute-start.13 = (bf16[320,256]{1,0:T(8,128)(2,1)}, bf16[320,256]{1,0:T(8,128)(2,1)S(1)}, u32[]{:S(2)}, u32[]{:S(2)}) collective-permute-start(bf16[320,256]{1,0:T(8,128)(2,1)} %get-tuple-element.47), channel_id=1, source_target_pairs={{0,12},{2,14},{4,0},{6,2},{8,4},{10,6},{12,8},{14,10},{1,13},{3,15... | collective-permute-start | bytes 491528 | tf_op jit(solution)/shard_map/ppermute | solution.py:52
  140.4 10.6 %collective-permute-done.15 = bf16[4,320,256]{2,1,0:T(8,128)(2,1)S(1)} collective-permute-done((bf16[4,320,256]{2,1,0:T(8,128)(2,1)S(1)}, bf16[4,320,256]{2,1,0:T(8,128)(2,1)S(1)}, u32[]{:S(2)}, u32[]{:S(2)}) %collective-permute-start.15) | collective-permute-done | bytes 655392 | tf_op jit(solution)/shard_map/ppermute | solution.py:41
  153.1 3.8 %collective-permute-start.18 = (bf16[320,256]{1,0:T(8,128)(2,1)}, bf16[320,256]{1,0:T(8,128)(2,1)}, u32[]{:S(2)}, u32[]{:S(2)}) collective-permute-start(bf16[320,256]{1,0:T(8,128)(2,1)} %get-tuple-element.50), channel_id=1, source_target_pairs={{0,12},{2,14},{4,0},{6,2},{8,4},{10,6},{12,8},{14,10},{1,13},{3,15... | collective-permute-start | bytes 491528 | tf_op jit(solution)/shard_map/ppermute | solution.py:52
  157.0 5.5 %collective-permute-done.16 = bf16[320,256]{1,0:T(8,128)(2,1)} collective-permute-done((bf16[320,256]{1,0:T(8,128)(2,1)}, bf16[320,256]{1,0:T(8,128)(2,1)}, u32[]{:S(2)}, u32[]{:S(2)}) %collective-permute-start.16) | collective-permute-done | bytes 163872 | tf_op jit(solution)/shard_map/ppermute | solution.py:52
  162.5 7.6 %collective-permute-done.17 = bf16[320,256]{1,0:T(8,128)(2,1)} collective-permute-done((bf16[320,256]{1,0:T(8,128)(2,1)}, bf16[320,256]{1,0:T(8,128)(2,1)}, u32[]{:S(2)}, u32[]{:S(2)}) %collective-permute-start.17) | collective-permute-done | bytes 163872 | tf_op jit(solution)/shard_map/ppermute | solution.py:52
  170.0 1.8 slice_subtract_fusion.3
  176.3 1.8 pad_maximum_fusion
  (96 shorter events, 31.1 us)
Async XLA Ops:
  7.2 62.4 %all-gather.2.cloned.1.call-start = ((), (), s32[]{:S(2)}) async-start(), calls=%async_computation | async-start | bytes 5570560 | tf_op jit(solution)/shard_map/all_gather | solution.py:27
  78.2 17.0 %collective-permute-start = (bf16[4,320,256]{2,1,0:T(8,128)(2,1)S(1)}, bf16[4,320,256]{2,1,0:T(8,128)(2,1)S(1)}, u32[]{:S(2)}, u32[]{:S(2)}) collective-permute-start(bf16[4,320,256]{2,1,0:T(8,128)(2,1)S(1)} %fusion.32), channel_id=1, source_target_pairs={{0,2},{2,0},{4,6},{6,4},{8,10},{10,8},{12,14},{14,12},{1,3},{3,1},... | collective-permute-start | bytes 1966088 | tf_op jit(solution)/shard_map/ppermute | solution.py:41
  95.4 16.1 %collective-permute-start.5 = (bf16[4,320,256]{2,1,0:T(8,128)(2,1)S(1)}, bf16[4,320,256]{2,1,0:T(8,128)(2,1)S(1)}, u32[]{:S(2)}, u32[]{:S(2)}) collective-permute-start(bf16[4,320,256]{2,1,0:T(8,128)(2,1)S(1)} %fusion.33), channel_id=1, source_target_pairs={{0,2},{2,0},{4,6},{6,4},{8,10},{10,8},{12,14},{14,12},{1,3},{3,1},... | collective-permute-start | bytes 1966088 | tf_op jit(solution)/shard_map/ppermute | solution.py:41
  98.6 14.2 %collective-permute-start.3 = (bf16[320,256]{1,0:T(8,128)(2,1)S(1)}, bf16[320,256]{1,0:T(8,128)(2,1)S(1)}, u32[]{:S(2)}, u32[]{:S(2)}) collective-permute-start(bf16[320,256]{1,0:T(8,128)(2,1)S(1)} %get-tuple-element.55), channel_id=1, source_target_pairs={{0,12},{2,14},{4,0},{6,2},{8,4},{10,6},{12,8},{14,10},{1,13},{3,15... | collective-permute-start | bytes 491528 | tf_op jit(solution)/shard_map/ppermute | solution.py:52
  100.6 14.8 %collective-permute-start.2 = (bf16[320,256]{1,0:T(8,128)(2,1)S(1)}, bf16[320,256]{1,0:T(8,128)(2,1)S(1)}, u32[]{:S(2)}, u32[]{:S(2)}) collective-permute-start(bf16[320,256]{1,0:T(8,128)(2,1)S(1)} %get-tuple-element.56), channel_id=1, source_target_pairs={{0,8},{2,10},{4,12},{6,14},{8,0},{10,2},{12,4},{14,6},{1,9},{3,11}... | collective-permute-start | bytes 491528 | tf_op jit(solution)/shard_map/ppermute | solution.py:52
  101.6 13.8 %collective-permute-start.1 = (bf16[320,256]{1,0:T(8,128)(2,1)S(1)}, bf16[320,256]{1,0:T(8,128)(2,1)S(1)}, u32[]{:S(2)}, u32[]{:S(2)}) collective-permute-start(bf16[320,256]{1,0:T(8,128)(2,1)S(1)} %get-tuple-element.57), channel_id=1, source_target_pairs={{0,4},{2,6},{4,8},{6,10},{8,12},{10,14},{12,0},{14,2},{1,5},{3,7},... | collective-permute-start | bytes 491528 | tf_op jit(solution)/shard_map/ppermute | solution.py:52
  115.4 14.6 %collective-permute-start.10 = (bf16[4,320,256]{2,1,0:T(8,128)(2,1)S(1)}, bf16[4,320,256]{2,1,0:T(8,128)(2,1)S(1)}, u32[]{:S(2)}, u32[]{:S(2)}) collective-permute-start(bf16[4,320,256]{2,1,0:T(8,128)(2,1)S(1)} %fusion.34), channel_id=1, source_target_pairs={{0,2},{2,0},{4,6},{6,4},{8,10},{10,8},{12,14},{14,12},{1,3},{3,1},... | collective-permute-start | bytes 1966088 | tf_op jit(solution)/shard_map/ppermute | solution.py:41
  118.7 11.5 %collective-permute-start.8 = (bf16[320,256]{1,0:T(8,128)(2,1)S(1)}, bf16[320,256]{1,0:T(8,128)(2,1)S(1)}, u32[]{:S(2)}, u32[]{:S(2)}) collective-permute-start(bf16[320,256]{1,0:T(8,128)(2,1)S(1)} %get-tuple-element.52), channel_id=1, source_target_pairs={{0,12},{2,14},{4,0},{6,2},{8,4},{10,6},{12,8},{14,10},{1,13},{3,15... | collective-permute-start | bytes 491528 | tf_op jit(solution)/shard_map/ppermute | solution.py:52
  118.7 16.5 %collective-permute-start.7 = (bf16[320,256]{1,0:T(8,128)(2,1)S(1)}, bf16[320,256]{1,0:T(8,128)(2,1)S(1)}, u32[]{:S(2)}, u32[]{:S(2)}) collective-permute-start(bf16[320,256]{1,0:T(8,128)(2,1)S(1)} %get-tuple-element.53), channel_id=1, source_target_pairs={{0,8},{2,10},{4,12},{6,14},{8,0},{10,2},{12,4},{14,6},{1,9},{3,11}... | collective-permute-start | bytes 491528 | tf_op jit(solution)/shard_map/ppermute | solution.py:52
  120.6 14.6 %collective-permute-start.6 = (bf16[320,256]{1,0:T(8,128)(2,1)S(1)}, bf16[320,256]{1,0:T(8,128)(2,1)S(1)}, u32[]{:S(2)}, u32[]{:S(2)}) collective-permute-start(bf16[320,256]{1,0:T(8,128)(2,1)S(1)} %get-tuple-element.54), channel_id=1, source_target_pairs={{0,4},{2,6},{4,8},{6,10},{8,12},{10,14},{12,0},{14,2},{1,5},{3,7},... | collective-permute-start | bytes 491528 | tf_op jit(solution)/shard_map/ppermute | solution.py:52
  130.2 22.1 %copy-start.3 = (bf16[320,256]{1,0:T(8,128)(2,1)}, bf16[320,256]{1,0:T(8,128)(2,1)S(1)}, u32[]{:S(2)}) copy-start(bf16[320,256]{1,0:T(8,128)(2,1)S(1)} %collective-permute-done.8) | copy-start | bytes 491524
  135.2 17.1 %copy-start.5 = (bf16[320,256]{1,0:T(8,128)(2,1)}, bf16[320,256]{1,0:T(8,128)(2,1)S(1)}, u32[]{:S(2)}) copy-start(bf16[320,256]{1,0:T(8,128)(2,1)S(1)} %collective-permute-done.7) | copy-start | bytes 491524
  135.2 17.1 %copy-start.7 = (bf16[320,256]{1,0:T(8,128)(2,1)}, bf16[320,256]{1,0:T(8,128)(2,1)S(1)}, u32[]{:S(2)}) copy-start(bf16[320,256]{1,0:T(8,128)(2,1)S(1)} %collective-permute-done.6) | copy-start | bytes 491524
  135.2 15.9 %collective-permute-start.15 = (bf16[4,320,256]{2,1,0:T(8,128)(2,1)S(1)}, bf16[4,320,256]{2,1,0:T(8,128)(2,1)S(1)}, u32[]{:S(2)}, u32[]{:S(2)}) collective-permute-start(bf16[4,320,256]{2,1,0:T(8,128)(2,1)S(1)} %fusion.35), channel_id=1, source_target_pairs={{0,2},{2,0},{4,6},{6,4},{8,10},{10,8},{12,14},{14,12},{1,3},{3,1},... | collective-permute-start | bytes 1966088 | tf_op jit(solution)/shard_map/ppermute | solution.py:41
  136.6 20.3 %collective-permute-start.11 = (bf16[320,256]{1,0:T(8,128)(2,1)S(1)}, bf16[320,256]{1,0:T(8,128)(2,1)S(1)}, u32[]{:S(2)}, u32[]{:S(2)}) collective-permute-start(bf16[320,256]{1,0:T(8,128)(2,1)S(1)} %get-tuple-element.46), channel_id=1, source_target_pairs={{0,4},{2,6},{4,8},{6,10},{8,12},{10,14},{12,0},{14,2},{1,5},{3,7},... | collective-permute-start | bytes 491528 | tf_op jit(solution)/shard_map/ppermute | solution.py:52
  136.6 20.3 %collective-permute-start.13 = (bf16[320,256]{1,0:T(8,128)(2,1)}, bf16[320,256]{1,0:T(8,128)(2,1)S(1)}, u32[]{:S(2)}, u32[]{:S(2)}) collective-permute-start(bf16[320,256]{1,0:T(8,128)(2,1)} %get-tuple-element.47), channel_id=1, source_target_pairs={{0,12},{2,14},{4,0},{6,2},{8,4},{10,6},{12,8},{14,10},{1,13},{3,15... | collective-permute-start | bytes 491528 | tf_op jit(solution)/shard_map/ppermute | solution.py:52
  140.4 16.5 %collective-permute-start.12 = (bf16[320,256]{1,0:T(8,128)(2,1)}, bf16[320,256]{1,0:T(8,128)(2,1)}, u32[]{:S(2)}, u32[]{:S(2)}) collective-permute-start(bf16[320,256]{1,0:T(8,128)(2,1)} %get-tuple-element.48), channel_id=1, source_target_pairs={{0,8},{2,10},{4,12},{6,14},{8,0},{10,2},{12,4},{14,6},{1,9},{3,11}... | collective-permute-start | bytes 491528 | tf_op jit(solution)/shard_map/ppermute | solution.py:52
  153.1 9.4 %collective-permute-start.16 = (bf16[320,256]{1,0:T(8,128)(2,1)}, bf16[320,256]{1,0:T(8,128)(2,1)}, u32[]{:S(2)}, u32[]{:S(2)}) collective-permute-start(bf16[320,256]{1,0:T(8,128)(2,1)} %get-tuple-element.49), channel_id=1, source_target_pairs={{0,4},{2,6},{4,8},{6,10},{8,12},{10,14},{12,0},{14,2},{1,5},{3,7},... | collective-permute-start | bytes 491528 | tf_op jit(solution)/shard_map/ppermute | solution.py:52
  153.1 9.4 %collective-permute-start.18 = (bf16[320,256]{1,0:T(8,128)(2,1)}, bf16[320,256]{1,0:T(8,128)(2,1)}, u32[]{:S(2)}, u32[]{:S(2)}) collective-permute-start(bf16[320,256]{1,0:T(8,128)(2,1)} %get-tuple-element.50), channel_id=1, source_target_pairs={{0,12},{2,14},{4,0},{6,2},{8,4},{10,6},{12,8},{14,10},{1,13},{3,15... | collective-permute-start | bytes 491528 | tf_op jit(solution)/shard_map/ppermute | solution.py:52
  156.9 13.1 %collective-permute-start.17 = (bf16[320,256]{1,0:T(8,128)(2,1)}, bf16[320,256]{1,0:T(8,128)(2,1)}, u32[]{:S(2)}, u32[]{:S(2)}) collective-permute-start(bf16[320,256]{1,0:T(8,128)(2,1)} %get-tuple-element.51), channel_id=1, source_target_pairs={{0,8},{2,10},{4,12},{6,14},{8,0},{10,2},{12,4},{14,6},{1,9},{3,11}... | collective-permute-start | bytes 491528 | tf_op jit(solution)/shard_map/ppermute | solution.py:52
  171.8 3.7 %collective-permute-start.4 = (f32[320,256]{1,0:T(8,128)S(1)}, f32[320,256]{1,0:T(8,128)S(1)}, u32[]{:S(2)}, u32[]{:S(2)}) collective-permute-start(f32[320,256]{1,0:T(8,128)S(1)} %get-tuple-element.15), channel_id=1, source_target_pairs={{0,1},{1,0},{2,3},{3,2},{4,5},{5,4},{6,7},{7,6},{8,9},{9,8},{10,11... | collective-permute-start | bytes 983048 | tf_op jit(solution)/shard_map/ppermute | solution.py:92
  173.3 2.3 %collective-permute-start.9 = (f32[320,256]{1,0:T(8,128)S(1)}, f32[320,256]{1,0:T(8,128)S(1)}, u32[]{:S(2)}, u32[]{:S(2)}) collective-permute-start(f32[320,256]{1,0:T(8,128)S(1)} %get-tuple-element.17), channel_id=1, source_target_pairs={{0,1},{1,0},{2,3},{3,2},{4,5},{5,4},{6,7},{7,6},{8,9},{9,8},{10,11... | collective-permute-start | bytes 983048 | tf_op jit(solution)/shard_map/ppermute | solution.py:92
  173.8 1.8 collective-permute-start.19
  173.9 2.1 %collective-permute-start.14 = (f32[320,256]{1,0:T(8,128)S(1)}, f32[320,256]{1,0:T(8,128)S(1)}, u32[]{:S(2)}, u32[]{:S(2)}) collective-permute-start(f32[320,256]{1,0:T(8,128)S(1)} %get-tuple-element.44), channel_id=1, source_target_pairs={{0,1},{1,0},{2,3},{3,2},{4,5},{5,4},{6,7},{7,6},{8,9},{9,8},{10,11... | collective-permute-start | bytes 983048 | tf_op jit(solution)/shard_map/ppermute | solution.py:92
  (10 other events, 32.5 us)
Sparse Core Ops, SparseCore 0:
  10.9 58.6 all-gather.1

commit v4 on v3

--- a/solution.py
+++ b/solution.py
@@ -20,11 +20,49 @@
     return result.reshape(count, width).astype(jnp.bfloat16)
 
 
-def gather_weight(weight):
+def in_order(pieces, me):
+    count = len(pieces)
+    stacked = jnp.stack(pieces[::-1] + pieces[:0:-1])
+    return lax.dynamic_slice_in_dim(stacked, count - 1 - me, count, 0)
+
+
+def gather_weight(weight, x_rows, cot_rows):
     weight_b = weight.astype(jnp.bfloat16)
-    rows = weight.shape[0] // lax.axis_size("clients")
-    own = lax.dynamic_slice_in_dim(weight_b, lax.axis_index("clients") * rows, rows, 0)
-    return lax.all_gather(own, ("fsdp", "clients"), axis=0, tiled=True)
+    members = lax.axis_size("clients")
+    core = lax.axis_index("clients")
+    rows = weight.shape[0] // members
+    own = lax.dynamic_slice_in_dim(weight_b, core * rows, rows, 0)
+    n = lax.axis_size("fsdp")
+    lines = n // 2
+    if lines > 4:
+        whole = lax.all_gather(own, ("fsdp", "clients"), axis=0, tiled=True)
+        return jnp.split(whole, 2, axis=1)
+    me = lax.axis_index("fsdp")
+    line, side = me // 2, lax.rem(me, 2)
+    halves = []
+    width = weight.shape[1] // 2
+    for half in range(2):
+        piece = own[:, half * width : (half + 1) * width]
+        if half:
+            piece = lax.optimization_barrier((piece, cot_rows, *pieces[1:]))[0]
+        pieces = [piece]
+        for step in range(1, lines):
+            pairs = [(i, (i + 2 * step) % n) for i in range(n)]
+            pieces.append(lax.ppermute(piece, "fsdp", pairs))
+        column = in_order(pieces, line)
+        if half:
+            column = lax.optimization_barrier((column, x_rows))[0]
+        other = lax.ppermute(column, "fsdp", [(i, i ^ 1) for i in range(n)])
+        first = jnp.where(side == 0, column, other)
+        second = jnp.where(side == 0, other, column)
+        plane = jnp.stack([first, second], axis=1)
+        cores = [plane]
+        for step in range(1, members):
+            pairs = [(i, (i + step) % members) for i in range(members)]
+            cores.append(lax.ppermute(plane, "clients", pairs))
+        ordered = in_order(cores, core)
+        halves.append(jnp.moveaxis(ordered, 0, 2).reshape(n * members * rows, width))
+    return halves
 
 
 def scatter_sum(partial, before):
@@ -63,18 +101,20 @@
 
 def per_device(pool_x, pool_cot, assignment, weight, gain, global_variate, client_variate):
     members = lax.axis_size("clients")
-    weight_b = gather_weight(weight)
     picked = assignment[0]
     x_rows = pool_x.at[picked].get(mode="promise_in_bounds")
     cot_rows = pool_cot.at[picked].get(mode="promise_in_bounds")
+    weight_b = gather_weight(weight, x_rows, cot_rows)
     width = weight.shape[1] // CHUNKS
     own_variate = client_variate[0]
     results, came, moved = [], [], []
     for chunk in range(CHUNKS):
         cut = slice(chunk * width, (chunk + 1) * width)
+        half, place = divmod(chunk, CHUNKS // 2)
         if chunk:
-            weight_b = lax.optimization_barrier((weight_b, sent))[0]
-        keys = jnp.dot(x_rows, weight_b[:, cut], preferred_element_type=jnp.float32)
+            weight_b[half] = lax.optimization_barrier((weight_b[half], sent))[0]
+        weight_c = weight_b[half][:, place * width : (place + 1) * width]
+        keys = jnp.dot(x_rows, weight_c, preferred_element_type=jnp.float32)
         dkeys = norm_backward(keys, cot_rows[:, cut], gain)
         partial = lax.dot_general(
             x_rows, dkeys, (((0,), (0,)), ((), ())), preferred_element_type=jnp.float32

time: 186 us -> 181 us (0.973)
  starting transfers between devices: 20.1 us -> 35.7 us
  between operations: 14.5 us -> 1.29 us
  waiting for transfers between devices: 79.6 us -> 69.8 us
  other arithmetic: 12.9 us -> 19.4 us
  matrix products: 15.8 us -> 12.8 us
    all_gather x1 -> x0, waiting for transfers between devices: 24.1 us -> none  [gather_weight(): return lax.all_gather(own, ('fsdp', 'clients'), axis=0, tiled=True)]
    ppermute x0 -> x10, waiting for transfers between devices: none -> 17.1 us  [the longest x2 8.55 us: gather_weight(): other = lax.ppermute(column, 'fsdp', [(i, i ^ 1) for i in range(n)])]
    ppermute x0 -> x10, starting transfers between devices: none -> 14 us  [the longest x6 10.9 us: gather_weight(): pieces.append(lax.ppermute(piece, 'fsdp', pairs))]
    another operation x0 -> x5, other arithmetic: none -> 5.85 us  [the longest x3 4.24 us: in_order(): stacked = jnp.stack(pieces[::-1] + pieces[:0:-1])]
    dot_general x4, matrix products: 9.46 us -> 6.6 us  [per_device(): keys = jnp.dot(x_rows, weight_c, preferred_element_type=jnp.float32)]
    ppermute x12, waiting for transfers between devices: 20.7 us -> 18.5 us  [scatter_sum(): got = lax.ppermute(block, 'fsdp', pairs)]
    unnamed x30 -> x48, local copies, waits for them, and re-layouts: 5.74 us -> 4.06 us
  transfers between devices with their start and end apart: 21 -> 30, of which waited for: 10 -> 12; matrix products, arithmetic and copies ran while one was open for 30% -> 37% of each run, Pallas kernels for 0% -> 0%
where the time goes in v4:
time: 181 us; the launch traced here: 180 us
  waiting for transfers between devices  69.8 us (39%)
  local copies, waits for them, and re-layouts  41.1 us (23%)
  starting transfers between devices  35.7 us (20%)
  other arithmetic  19.4 us (11%)
  matrix products  12.8 us (7%)
    ppermute x4, waiting for transfers between devices, scatter_sum(): came = lax.ppermute(ready, 'fsdp', [(i, i ^ 1) for i in range(n)])  34.2 us
    ppermute x12, waiting for transfers between devices, scatter_sum(): got = lax.ppermute(block, 'fsdp', pairs)  18.5 us
    gather x1, local copies, waits for them, and re-layouts, per_device(): x_rows = pool_x.at[picked].get(mode='promise_in_bounds')  15.8 us
    ppermute x12, starting transfers between devices, scatter_sum(): got = lax.ppermute(block, 'fsdp', pairs)  15.4 us
    ppermute x6, starting transfers between devices, gather_weight(): pieces.append(lax.ppermute(piece, 'fsdp', pairs))  10.9 us
    ppermute x2, waiting for transfers between devices, gather_weight(): other = lax.ppermute(column, 'fsdp', [(i, i ^ 1) for i in range(n)])  8.55 us
    ppermute x6, waiting for transfers between devices, gather_weight(): pieces.append(lax.ppermute(piece, 'fsdp', pairs))  8.5 us
    dot_general x1, local copies, waits for them, and re-layouts, per_device(): lax.dot_general(x_rows, dkeys, (((0,), (0,)), ((), ())), preferred_elemen...  7.95 us
  transfers between devices with their start and end apart: 30, of which 12 were waited for; matrix products, arithmetic and copies ran while one was open for 37% of the time, Pallas kernels for 0%

profile of v4, /device:TPU:0, one launch (start us, length us, event | category | flops | bytes accessed | tf_op | source)
XLA Modules:
  0.0 180.1 jit_solution(5362203316244017228)
XLA Ops:
  1.8 3.1 %collective-permute-start.2 = (bf16[160,512]{1,0:T(8,128)(2,1)S(1)}, bf16[160,512]{1,0:T(8,128)(2,1)S(1)}, u32[]{:S(2)}, u32[]{:S(2)}) collective-permute-start(bf16[160,512]{1,0:T(8,128)(2,1)S(1)} %get-tuple-element.70), channel_id=1, source_target_pairs={{0,4},{2,6},{4,8},{6,10},{8,12},{10,14},{12,0},{14,2},{1,5},{3,7},... | collective-permute-start | bytes 491528 | tf_op jit(solution)/shard_map/ppermute | solution.py:51
  4.9 2.6 %collective-permute-start.1 = (bf16[160,512]{1,0:T(8,128)(2,1)S(1)}, bf16[160,512]{1,0:T(8,128)(2,1)S(1)}, u32[]{:S(2)}, u32[]{:S(2)}) collective-permute-start(bf16[160,512]{1,0:T(8,128)(2,1)S(1)} %get-tuple-element.70), channel_id=1, source_target_pairs={{0,8},{2,10},{4,12},{6,14},{8,0},{10,2},{12,4},{14,6},{1,9},{3,11}... | collective-permute-start | bytes 491528 | tf_op jit(solution)/shard_map/ppermute | solution.py:51
  8.9 7.7 %gather_fusion.1 = bf16[1024,1024]{1,0:T(8,128)(2,1)S(1)} fusion(bf16[2048,1024]{1,0:T(8,128)(2,1)} %param.8, s32[1024]{0:T(1024)S(1)} %broadcast_clamp_fusion), kind=kCustom, calls=%fused_computation.1 | custom fusion | bytes 4198400 | tf_op jit(solution)/shard_map/gather | solution.py:106
  16.6 15.8 %gather_fusion = bf16[1024,2560]{1,0:T(8,128)(2,1)} fusion(bf16[2048,2560]{1,0:T(8,128)(2,1)} %param.7, s32[1024]{0:T(1024)S(1)} %broadcast_clamp_fusion), kind=kCustom, calls=%fused_computation | custom fusion | bytes 10489856 | tf_op jit(solution)/shard_map/gather | solution.py:105
  33.4 2.8 %collective-permute-start.15 = (bf16[160,512]{1,0:T(8,128)(2,1)S(1)}, bf16[160,512]{1,0:T(8,128)(2,1)S(1)}, u32[]{:S(2)}, u32[]{:S(2)}) collective-permute-start(bf16[160,512]{1,0:T(8,128)(2,1)S(1)} %get-tuple-element.13), channel_id=1, source_target_pairs={{0,12},{2,14},{4,0},{6,2},{8,4},{10,6},{12,8},{14,10},{1,13},{3,15... | collective-permute-start | bytes 491528 | tf_op jit(solution)/shard_map/ppermute | solution.py:51
  38.0 6.6 %collective-permute-done.15 = bf16[160,512]{1,0:T(8,128)(2,1)S(1)} collective-permute-done((bf16[160,512]{1,0:T(8,128)(2,1)S(1)}, bf16[160,512]{1,0:T(8,128)(2,1)S(1)}, u32[]{:S(2)}, u32[]{:S(2)}) %collective-permute-start.15) | collective-permute-done | bytes 163872 | tf_op jit(solution)/shard_map/ppermute | solution.py:51
  44.7 1.9 %collective-permute-done.16 = bf16[160,512]{1,0:T(8,128)(2,1)S(1)} collective-permute-done((bf16[160,512]{1,0:T(8,128)(2,1)S(1)}, bf16[160,512]{1,0:T(8,128)(2,1)S(1)}, u32[]{:S(2)}, u32[]{:S(2)}) %collective-permute-start.16) | collective-permute-done | bytes 163872 | tf_op jit(solution)/shard_map/ppermute | solution.py:51
  46.6 5.0 %collective-permute-done.3 = bf16[4,160,512]{2,1,0:T(8,128)(2,1)S(1)} collective-permute-done((bf16[4,160,512]{2,1,0:T(8,128)(2,1)S(1)}, bf16[4,160,512]{2,1,0:T(8,128)(2,1)S(1)}, u32[]{:S(2)}, u32[]{:S(2)}) %collective-permute-start.3) | collective-permute-done | bytes 655392 | tf_op jit(solution)/shard_map/ppermute | solution.py:55
  59.7 8.0 %copy.22 = bf16[2560,1024]{1,0:T(8,128)(2,1)} copy(bf16[2560,1024]{0,1:T(8,128)(2,1)} %bitcast.256) | data formatting | bytes 10485760 | tf_op jit(solution)/shard_map/dot_general | solution.py:119
  67.7 3.6 %collective-permute-done.18 = bf16[4,160,512]{2,1,0:T(8,128)(2,1)} collective-permute-done((bf16[4,160,512]{2,1,0:T(8,128)(2,1)}, bf16[4,160,512]{2,1,0:T(8,128)(2,1)}, u32[]{:S(2)}, u32[]{:S(2)}) %collective-permute-start.18) | collective-permute-done | bytes 655392 | tf_op jit(solution)/shard_map/ppermute | solution.py:55
  73.1 2.8 %fusion.8 = bf16[2,4,2,160,512]{4,3,0,2,1:T(8,128)(2,1)S(1)} fusion(s32[]{:T(128)S(6)} %select_n.97, bf16[1,4,2,160,512]{4,3,0,2,1:T(8,128)(2,1)} %bitcast.12, bf16[1,4,2,160,512]{4,3,0,2,1:T(8,128)(2,1)S(1)} %get-tuple-element.50), kind=kLoop, calls=%fused_computation.16 | loop fusion | flops 2621440 | bytes 5242884 | tf_op jit(solution)/shard_map/stack | solution.py:25
  87.1 1.8 %multiply_reduce_fusion.3 = (f32[1024,2]{0,1:T(2,128)S(1)}, f32[1024,256]{0,1:T(8,128)S(1)}) fusion(bf16[1024,2560]{1,0:T(8,128)(2,1)S(1)} %bitcast.258, bf16[2560,512]{1,0:T(8,128)(2,1)S(1)} %bitcast.273), kind=kOutput, calls=%fused_computation.75 | convolution fusion | flops 1342699520 | bytes 7610368 | tf_op jit(solution)/shard_map/dot_general | solution.py:117
  91.3 6.2 %collective-permute-done.5 = bf16[4,320,256]{2,1,0:T(8,128)(2,1)S(1)} collective-permute-done((bf16[4,320,256]{2,1,0:T(8,128)(2,1)S(1)}, bf16[4,320,256]{2,1,0:T(8,128)(2,1)S(1)}, u32[]{:S(2)}, u32[]{:S(2)}) %collective-permute-start.5) | collective-permute-done | bytes 655392 | tf_op jit(solution)/shard_map/ppermute | solution.py:79
  105.4 9.0 %collective-permute-done.10 = bf16[4,320,256]{2,1,0:T(8,128)(2,1)S(1)} collective-permute-done((bf16[4,320,256]{2,1,0:T(8,128)(2,1)S(1)}, bf16[4,320,256]{2,1,0:T(8,128)(2,1)S(1)}, u32[]{:S(2)}, u32[]{:S(2)}) %collective-permute-start.10) | collective-permute-done | bytes 655392 | tf_op jit(solution)/shard_map/ppermute | solution.py:79
  115.6 2.4 %collective-permute-done.7 = bf16[320,256]{1,0:T(8,128)(2,1)S(1)} collective-permute-done((bf16[320,256]{1,0:T(8,128)(2,1)S(1)}, bf16[320,256]{1,0:T(8,128)(2,1)S(1)}, u32[]{:S(2)}, u32[]{:S(2)}) %collective-permute-start.7) | collective-permute-done | bytes 163872 | tf_op jit(solution)/shard_map/ppermute | solution.py:90
  120.3 1.9 %collective-permute-start.12 = (bf16[320,256]{1,0:T(8,128)(2,1)S(1)}, bf16[320,256]{1,0:T(8,128)(2,1)S(1)}, u32[]{:S(2)}, u32[]{:S(2)}) collective-permute-start(bf16[320,256]{1,0:T(8,128)(2,1)S(1)} %get-tuple-element.65), channel_id=1, source_target_pairs={{0,8},{2,10},{4,12},{6,14},{8,0},{10,2},{12,4},{14,6},{1,9},{3,11}... | collective-permute-start | bytes 491528 | tf_op jit(solution)/shard_map/ppermute | solution.py:90
  122.2 1.9 %collective-permute-start.11 = (bf16[320,256]{1,0:T(8,128)(2,1)S(1)}, bf16[320,256]{1,0:T(8,128)(2,1)S(1)}, u32[]{:S(2)}, u32[]{:S(2)}) collective-permute-start(bf16[320,256]{1,0:T(8,128)(2,1)S(1)} %get-tuple-element.66), channel_id=1, source_target_pairs={{0,4},{2,6},{4,8},{6,10},{8,12},{10,14},{12,0},{14,2},{1,5},{3,7},... | collective-permute-start | bytes 491528 | tf_op jit(solution)/shard_map/ppermute | solution.py:90
  124.2 9.3 %collective-permute-done.20 = bf16[4,320,256]{2,1,0:T(8,128)(2,1)S(1)} collective-permute-done((bf16[4,320,256]{2,1,0:T(8,128)(2,1)S(1)}, bf16[4,320,256]{2,1,0:T(8,128)(2,1)S(1)}, u32[]{:S(2)}, u32[]{:S(2)}) %collective-permute-start.20) | collective-permute-done | bytes 655392 | tf_op jit(solution)/shard_map/ppermute | solution.py:79
  133.7 3.1 %collective-permute-done.12 = bf16[320,256]{1,0:T(8,128)(2,1)S(1)} collective-permute-done((bf16[320,256]{1,0:T(8,128)(2,1)S(1)}, bf16[320,256]{1,0:T(8,128)(2,1)S(1)}, u32[]{:S(2)}, u32[]{:S(2)}) %collective-permute-start.12) | collective-permute-done | bytes 163872 | tf_op jit(solution)/shard_map/ppermute | solution.py:90
  139.1 3.8 %collective-permute-start.23 = (bf16[320,256]{1,0:T(8,128)(2,1)}, bf16[320,256]{1,0:T(8,128)(2,1)S(1)}, u32[]{:S(2)}, u32[]{:S(2)}) collective-permute-start(bf16[320,256]{1,0:T(8,128)(2,1)} %get-tuple-element.59), channel_id=1, source_target_pairs={{0,12},{2,14},{4,0},{6,2},{8,4},{10,6},{12,8},{14,10},{1,13},{3,15... | collective-permute-start | bytes 491528 | tf_op jit(solution)/shard_map/ppermute | solution.py:90
  142.9 9.7 %collective-permute-done.25 = bf16[4,320,256]{2,1,0:T(8,128)(2,1)S(1)} collective-permute-done((bf16[4,320,256]{2,1,0:T(8,128)(2,1)S(1)}, bf16[4,320,256]{2,1,0:T(8,128)(2,1)S(1)}, u32[]{:S(2)}, u32[]{:S(2)}) %collective-permute-start.25) | collective-permute-done | bytes 655392 | tf_op jit(solution)/shard_map/ppermute | solution.py:79
  154.7 3.8 %collective-permute-start.28 = (bf16[320,256]{1,0:T(8,128)(2,1)}, bf16[320,256]{1,0:T(8,128)(2,1)}, u32[]{:S(2)}, u32[]{:S(2)}) collective-permute-start(bf16[320,256]{1,0:T(8,128)(2,1)} %get-tuple-element.62), channel_id=1, source_target_pairs={{0,12},{2,14},{4,0},{6,2},{8,4},{10,6},{12,8},{14,10},{1,13},{3,15... | collective-permute-start | bytes 491528 | tf_op jit(solution)/shard_map/ppermute | solution.py:90
  158.6 5.5 %collective-permute-done.26 = bf16[320,256]{1,0:T(8,128)(2,1)} collective-permute-done((bf16[320,256]{1,0:T(8,128)(2,1)}, bf16[320,256]{1,0:T(8,128)(2,1)}, u32[]{:S(2)}, u32[]{:S(2)}) %collective-permute-start.26) | collective-permute-done | bytes 163872 | tf_op jit(solution)/shard_map/ppermute | solution.py:90
  164.1 7.6 %collective-permute-done.27 = bf16[320,256]{1,0:T(8,128)(2,1)} collective-permute-done((bf16[320,256]{1,0:T(8,128)(2,1)}, bf16[320,256]{1,0:T(8,128)(2,1)}, u32[]{:S(2)}, u32[]{:S(2)}) %collective-permute-start.27) | collective-permute-done | bytes 163872 | tf_op jit(solution)/shard_map/ppermute | solution.py:90
  (144 shorter events, 53.0 us)
Async XLA Ops:
  1.8 30.6 %collective-permute-start.2 = (bf16[160,512]{1,0:T(8,128)(2,1)S(1)}, bf16[160,512]{1,0:T(8,128)(2,1)S(1)}, u32[]{:S(2)}, u32[]{:S(2)}) collective-permute-start(bf16[160,512]{1,0:T(8,128)(2,1)S(1)} %get-tuple-element.70), channel_id=1, source_target_pairs={{0,4},{2,6},{4,8},{6,10},{8,12},{10,14},{12,0},{14,2},{1,5},{3,7},... | collective-permute-start | bytes 491528 | tf_op jit(solution)/shard_map/ppermute | solution.py:51
  4.9 27.5 %collective-permute-start.1 = (bf16[160,512]{1,0:T(8,128)(2,1)S(1)}, bf16[160,512]{1,0:T(8,128)(2,1)S(1)}, u32[]{:S(2)}, u32[]{:S(2)}) collective-permute-start(bf16[160,512]{1,0:T(8,128)(2,1)S(1)} %get-tuple-element.70), channel_id=1, source_target_pairs={{0,8},{2,10},{4,12},{6,14},{8,0},{10,2},{12,4},{14,6},{1,9},{3,11}... | collective-permute-start | bytes 491528 | tf_op jit(solution)/shard_map/ppermute | solution.py:51
  7.5 24.9 %collective-permute-start = (bf16[160,512]{1,0:T(8,128)(2,1)S(1)}, bf16[160,512]{1,0:T(8,128)(2,1)S(1)}, u32[]{:S(2)}, u32[]{:S(2)}) collective-permute-start(bf16[160,512]{1,0:T(8,128)(2,1)S(1)} %get-tuple-element.70), channel_id=1, source_target_pairs={{0,12},{2,14},{4,0},{6,2},{8,4},{10,6},{12,8},{14,10},{1,13},{3,15... | collective-permute-start | bytes 491528 | tf_op jit(solution)/shard_map/ppermute | solution.py:51
  32.4 14.2 %collective-permute-start.17 = (bf16[160,512]{1,0:T(8,128)(2,1)S(1)}, bf16[160,512]{1,0:T(8,128)(2,1)S(1)}, u32[]{:S(2)}, u32[]{:S(2)}) collective-permute-start(bf16[160,512]{1,0:T(8,128)(2,1)S(1)} %get-tuple-element.13), channel_id=1, source_target_pairs={{0,4},{2,6},{4,8},{6,10},{8,12},{10,14},{12,0},{14,2},{1,5},{3,7},... | collective-permute-start | bytes 491528 | tf_op jit(solution)/shard_map/ppermute | solution.py:51
  33.1 13.4 %collective-permute-start.16 = (bf16[160,512]{1,0:T(8,128)(2,1)S(1)}, bf16[160,512]{1,0:T(8,128)(2,1)S(1)}, u32[]{:S(2)}, u32[]{:S(2)}) collective-permute-start(bf16[160,512]{1,0:T(8,128)(2,1)S(1)} %get-tuple-element.13), channel_id=1, source_target_pairs={{0,8},{2,10},{4,12},{6,14},{8,0},{10,2},{12,4},{14,6},{1,9},{3,11}... | collective-permute-start | bytes 491528 | tf_op jit(solution)/shard_map/ppermute | solution.py:51
  33.4 11.2 %collective-permute-start.15 = (bf16[160,512]{1,0:T(8,128)(2,1)S(1)}, bf16[160,512]{1,0:T(8,128)(2,1)S(1)}, u32[]{:S(2)}, u32[]{:S(2)}) collective-permute-start(bf16[160,512]{1,0:T(8,128)(2,1)S(1)} %get-tuple-element.13), channel_id=1, source_target_pairs={{0,12},{2,14},{4,0},{6,2},{8,4},{10,6},{12,8},{14,10},{1,13},{3,15... | collective-permute-start | bytes 491528 | tf_op jit(solution)/shard_map/ppermute | solution.py:51
  36.5 15.1 %collective-permute-start.3 = (bf16[4,160,512]{2,1,0:T(8,128)(2,1)S(1)}, bf16[4,160,512]{2,1,0:T(8,128)(2,1)S(1)}, u32[]{:S(2)}, u32[]{:S(2)}) collective-permute-start(bf16[4,160,512]{2,1,0:T(8,128)(2,1)S(1)} %constant_dynamic-slice_fusion.1), channel_id=1, source_target_pairs={{0,2},{2,0},{4,6},{6,4},{8,10},{10,8},{12,14},{14,12},{1,3},{3,1},... | collective-permute-start | bytes 1966088 | tf_op jit(solution)/shard_map/ppermute | solution.py:55
  52.9 20.2 %collective-permute-start.4 = (bf16[4,2,160,512]{3,2,1,0:T(8,128)(2,1)}, bf16[4,2,160,512]{3,2,1,0:T(8,128)(2,1)}, u32[]{:S(2)}, u32[]{:S(2)}) collective-permute-start(bf16[4,2,160,512]{3,2,1,0:T(8,128)(2,1)} %get-tuple-element.51), channel_id=1, source_target_pairs={{0,1},{1,0},{2,3},{3,2},{4,5},{5,4},{6,7},{7,6},{8,9},{9,8},{10,11... | collective-permute-start | bytes 3932168 | tf_op jit(solution)/shard_map/ppermute | solution.py:62
  53.8 17.5 %collective-permute-start.18 = (bf16[4,160,512]{2,1,0:T(8,128)(2,1)}, bf16[4,160,512]{2,1,0:T(8,128)(2,1)}, u32[]{:S(2)}, u32[]{:S(2)}) collective-permute-start(bf16[4,160,512]{2,1,0:T(8,128)(2,1)} %constant_dynamic-slice_fusion), channel_id=1, source_target_pairs={{0,2},{2,0},{4,6},{6,4},{8,10},{10,8},{12,14},{14,12},{1,3},{3,1},... | collective-permute-start | bytes 1966088 | tf_op jit(solution)/shard_map/ppermute | solution.py:55
  73.0 12.5 %collective-permute-start.19 = (bf16[4,2,160,512]{3,2,0,1:T(8,128)(2,1)S(1)}, bf16[4,2,160,512]{3,2,0,1:T(8,128)(2,1)S(1)}, u32[]{:S(2)}, u32[]{:S(2)}) collective-permute-start(bf16[4,2,160,512]{3,2,0,1:T(8,128)(2,1)S(1)} %get-tuple-element.55), channel_id=1, source_target_pairs={{0,1},{1,0},{2,3},{3,2},{4,5},{5,4},{6,7},{7,6},{8,9},{9,8},{10,11... | collective-permute-start | bytes 3932168 | tf_op jit(solution)/shard_map/ppermute | solution.py:62
  80.0 17.5 %collective-permute-start.5 = (bf16[4,320,256]{2,1,0:T(8,128)(2,1)S(1)}, bf16[4,320,256]{2,1,0:T(8,128)(2,1)S(1)}, u32[]{:S(2)}, u32[]{:S(2)}) collective-permute-start(bf16[4,320,256]{2,1,0:T(8,128)(2,1)S(1)} %fusion.37), channel_id=1, source_target_pairs={{0,2},{2,0},{4,6},{6,4},{8,10},{10,8},{12,14},{14,12},{1,3},{3,1},... | collective-permute-start | bytes 1966088 | tf_op jit(solution)/shard_map/ppermute | solution.py:79
  97.7 16.7 %collective-permute-start.10 = (bf16[4,320,256]{2,1,0:T(8,128)(2,1)S(1)}, bf16[4,320,256]{2,1,0:T(8,128)(2,1)S(1)}, u32[]{:S(2)}, u32[]{:S(2)}) collective-permute-start(bf16[4,320,256]{2,1,0:T(8,128)(2,1)S(1)} %fusion.38), channel_id=1, source_target_pairs={{0,2},{2,0},{4,6},{6,4},{8,10},{10,8},{12,14},{14,12},{1,3},{3,1},... | collective-permute-start | bytes 1966088 | tf_op jit(solution)/shard_map/ppermute | solution.py:79
  101.6 14.0 %collective-permute-start.8 = (bf16[320,256]{1,0:T(8,128)(2,1)S(1)}, bf16[320,256]{1,0:T(8,128)(2,1)S(1)}, u32[]{:S(2)}, u32[]{:S(2)}) collective-permute-start(bf16[320,256]{1,0:T(8,128)(2,1)S(1)} %get-tuple-element.67), channel_id=1, source_target_pairs={{0,12},{2,14},{4,0},{6,2},{8,4},{10,6},{12,8},{14,10},{1,13},{3,15... | collective-permute-start | bytes 491528 | tf_op jit(solution)/shard_map/ppermute | solution.py:90
  102.6 15.4 %collective-permute-start.7 = (bf16[320,256]{1,0:T(8,128)(2,1)S(1)}, bf16[320,256]{1,0:T(8,128)(2,1)S(1)}, u32[]{:S(2)}, u32[]{:S(2)}) collective-permute-start(bf16[320,256]{1,0:T(8,128)(2,1)S(1)} %get-tuple-element.68), channel_id=1, source_target_pairs={{0,8},{2,10},{4,12},{6,14},{8,0},{10,2},{12,4},{14,6},{1,9},{3,11}... | collective-permute-start | bytes 491528 | tf_op jit(solution)/shard_map/ppermute | solution.py:90
  103.7 14.3 %collective-permute-start.6 = (bf16[320,256]{1,0:T(8,128)(2,1)S(1)}, bf16[320,256]{1,0:T(8,128)(2,1)S(1)}, u32[]{:S(2)}, u32[]{:S(2)}) collective-permute-start(bf16[320,256]{1,0:T(8,128)(2,1)S(1)} %get-tuple-element.69), channel_id=1, source_target_pairs={{0,4},{2,6},{4,8},{6,10},{8,12},{10,14},{12,0},{14,2},{1,5},{3,7},... | collective-permute-start | bytes 491528 | tf_op jit(solution)/shard_map/ppermute | solution.py:90
  118.0 15.4 %collective-permute-start.20 = (bf16[4,320,256]{2,1,0:T(8,128)(2,1)S(1)}, bf16[4,320,256]{2,1,0:T(8,128)(2,1)S(1)}, u32[]{:S(2)}, u32[]{:S(2)}) collective-permute-start(bf16[4,320,256]{2,1,0:T(8,128)(2,1)S(1)} %fusion.39), channel_id=1, source_target_pairs={{0,2},{2,0},{4,6},{6,4},{8,10},{10,8},{12,14},{14,12},{1,3},{3,1},... | collective-permute-start | bytes 1966088 | tf_op jit(solution)/shard_map/ppermute | solution.py:79
  120.2 13.4 %collective-permute-start.13 = (bf16[320,256]{1,0:T(8,128)(2,1)S(1)}, bf16[320,256]{1,0:T(8,128)(2,1)S(1)}, u32[]{:S(2)}, u32[]{:S(2)}) collective-permute-start(bf16[320,256]{1,0:T(8,128)(2,1)S(1)} %get-tuple-element.64), channel_id=1, source_target_pairs={{0,12},{2,14},{4,0},{6,2},{8,4},{10,6},{12,8},{14,10},{1,13},{3,15... | collective-permute-start | bytes 491528 | tf_op jit(solution)/shard_map/ppermute | solution.py:90
  120.3 16.5 %collective-permute-start.12 = (bf16[320,256]{1,0:T(8,128)(2,1)S(1)}, bf16[320,256]{1,0:T(8,128)(2,1)S(1)}, u32[]{:S(2)}, u32[]{:S(2)}) collective-permute-start(bf16[320,256]{1,0:T(8,128)(2,1)S(1)} %get-tuple-element.65), channel_id=1, source_target_pairs={{0,8},{2,10},{4,12},{6,14},{8,0},{10,2},{12,4},{14,6},{1,9},{3,11}... | collective-permute-start | bytes 491528 | tf_op jit(solution)/shard_map/ppermute | solution.py:90
  122.2 14.6 %collective-permute-start.11 = (bf16[320,256]{1,0:T(8,128)(2,1)S(1)}, bf16[320,256]{1,0:T(8,128)(2,1)S(1)}, u32[]{:S(2)}, u32[]{:S(2)}) collective-permute-start(bf16[320,256]{1,0:T(8,128)(2,1)S(1)} %get-tuple-element.66), channel_id=1, source_target_pairs={{0,4},{2,6},{4,8},{6,10},{8,12},{10,14},{12,0},{14,2},{1,5},{3,7},... | collective-permute-start | bytes 491528 | tf_op jit(solution)/shard_map/ppermute | solution.py:90
  136.8 15.9 %collective-permute-start.25 = (bf16[4,320,256]{2,1,0:T(8,128)(2,1)S(1)}, bf16[4,320,256]{2,1,0:T(8,128)(2,1)S(1)}, u32[]{:S(2)}, u32[]{:S(2)}) collective-permute-start(bf16[4,320,256]{2,1,0:T(8,128)(2,1)S(1)} %fusion.40), channel_id=1, source_target_pairs={{0,2},{2,0},{4,6},{6,4},{8,10},{10,8},{12,14},{14,12},{1,3},{3,1},... | collective-permute-start | bytes 1966088 | tf_op jit(solution)/shard_map/ppermute | solution.py:79
  139.1 19.4 %collective-permute-start.21 = (bf16[320,256]{1,0:T(8,128)(2,1)S(1)}, bf16[320,256]{1,0:T(8,128)(2,1)S(1)}, u32[]{:S(2)}, u32[]{:S(2)}) collective-permute-start(bf16[320,256]{1,0:T(8,128)(2,1)S(1)} %get-tuple-element.58), channel_id=1, source_target_pairs={{0,4},{2,6},{4,8},{6,10},{8,12},{10,14},{12,0},{14,2},{1,5},{3,7},... | collective-permute-start | bytes 491528 | tf_op jit(solution)/shard_map/ppermute | solution.py:90
  139.1 19.4 %collective-permute-start.23 = (bf16[320,256]{1,0:T(8,128)(2,1)}, bf16[320,256]{1,0:T(8,128)(2,1)S(1)}, u32[]{:S(2)}, u32[]{:S(2)}) collective-permute-start(bf16[320,256]{1,0:T(8,128)(2,1)} %get-tuple-element.59), channel_id=1, source_target_pairs={{0,12},{2,14},{4,0},{6,2},{8,4},{10,6},{12,8},{14,10},{1,13},{3,15... | collective-permute-start | bytes 491528 | tf_op jit(solution)/shard_map/ppermute | solution.py:90
  142.9 15.6 %collective-permute-start.22 = (bf16[320,256]{1,0:T(8,128)(2,1)}, bf16[320,256]{1,0:T(8,128)(2,1)}, u32[]{:S(2)}, u32[]{:S(2)}) collective-permute-start(bf16[320,256]{1,0:T(8,128)(2,1)} %get-tuple-element.60), channel_id=1, source_target_pairs={{0,8},{2,10},{4,12},{6,14},{8,0},{10,2},{12,4},{14,6},{1,9},{3,11}... | collective-permute-start | bytes 491528 | tf_op jit(solution)/shard_map/ppermute | solution.py:90
  158.5 13.1 %collective-permute-start.27 = (bf16[320,256]{1,0:T(8,128)(2,1)}, bf16[320,256]{1,0:T(8,128)(2,1)}, u32[]{:S(2)}, u32[]{:S(2)}) collective-permute-start(bf16[320,256]{1,0:T(8,128)(2,1)} %get-tuple-element.63), channel_id=1, source_target_pairs={{0,8},{2,10},{4,12},{6,14},{8,0},{10,2},{12,4},{14,6},{1,9},{3,11}... | collective-permute-start | bytes 491528 | tf_op jit(solution)/shard_map/ppermute | solution.py:90
  (22 other events, 128.5 us)

commit v5 on v4

--- a/solution.py
+++ b/solution.py
@@ -26,7 +26,7 @@
     return lax.dynamic_slice_in_dim(stacked, count - 1 - me, count, 0)
 
 
-def gather_weight(weight, x_rows, cot_rows):
+def gather_weight(weight, x_rows):
     weight_b = weight.astype(jnp.bfloat16)
     members = lax.axis_size("clients")
     core = lax.axis_index("clients")
@@ -43,15 +43,13 @@
     width = weight.shape[1] // 2
     for half in range(2):
         piece = own[:, half * width : (half + 1) * width]
-        if half:
-            piece = lax.optimization_barrier((piece, cot_rows, *pieces[1:]))[0]
         pieces = [piece]
         for step in range(1, lines):
             pairs = [(i, (i + 2 * step) % n) for i in range(n)]
             pieces.append(lax.ppermute(piece, "fsdp", pairs))
         column = in_order(pieces, line)
         if half:
-            column = lax.optimization_barrier((column, x_rows))[0]
+            column = lax.optimization_barrier((column, x_rows, other))[0]
         other = lax.ppermute(column, "fsdp", [(i, i ^ 1) for i in range(n)])
         first = jnp.where(side == 0, column, other)
         second = jnp.where(side == 0, other, column)
@@ -104,7 +102,7 @@
     picked = assignment[0]
     x_rows = pool_x.at[picked].get(mode="promise_in_bounds")
     cot_rows = pool_cot.at[picked].get(mode="promise_in_bounds")
-    weight_b = gather_weight(weight, x_rows, cot_rows)
+    weight_b = gather_weight(weight, x_rows)
     width = weight.shape[1] // CHUNKS
     own_variate = client_variate[0]
     results, came, moved = [], [], []

time: 181 us -> 186 us (1.028)
  waiting for transfers between devices: 69.8 us -> 72.7 us
    ppermute x6, waiting for transfers between devices: 8.5 us -> 22.3 us  [gather_weight(): pieces.append(lax.ppermute(piece, 'fsdp', pairs))]
    ppermute x2, waiting for transfers between devices: 8.55 us -> 0.01 us  [gather_weight(): other = lax.ppermute(column, 'fsdp', [(i, i ^ 1) for i in range(n)])]
    ppermute x12, waiting for transfers between devices: 18.5 us -> 13.3 us  [scatter_sum(): got = lax.ppermute(block, 'fsdp', pairs)]
    unnamed x48 -> x58, local copies, waits for them, and re-layouts: 4.06 us -> 6.34 us
    ppermute x4, waiting for transfers between devices: 34.2 us -> 36.4 us  [scatter_sum(): came = lax.ppermute(ready, 'fsdp', [(i, i ^ 1) for i in range(n)])]
  transfers between devices with their start and end apart: 30 -> 30, of which waited for: 12 -> 12; matrix products, arithmetic and copies ran while one was open for 37% -> 36% of each run, Pallas kernels for 0% -> 0%
where the time goes in v5:
time: 186 us; the launch traced here: 185 us
  waiting for transfers between devices  72.7 us (39%)
  local copies, waits for them, and re-layouts  42 us (23%)
  starting transfers between devices  35.6 us (19%)
  other arithmetic  20.9 us (11%)
  matrix products  12.7 us (7%)
    ppermute x4, waiting for transfers between devices, scatter_sum(): came = lax.ppermute(ready, 'fsdp', [(i, i ^ 1) for i in range(n)])  36.4 us
    ppermute x6, waiting for transfers between devices, gather_weight(): pieces.append(lax.ppermute(piece, 'fsdp', pairs))  22.3 us
    ppermute x12, starting transfers between devices, scatter_sum(): got = lax.ppermute(block, 'fsdp', pairs)  16.8 us
    gather x1, local copies, waits for them, and re-layouts, per_device(): x_rows = pool_x.at[picked].get(mode='promise_in_bounds')  15.8 us
    ppermute x12, waiting for transfers between devices, scatter_sum(): got = lax.ppermute(block, 'fsdp', pairs)  13.3 us
    ppermute x6, starting transfers between devices, gather_weight(): pieces.append(lax.ppermute(piece, 'fsdp', pairs))  10.7 us
    dot_general x1, local copies, waits for them, and re-layouts, per_device(): lax.dot_general(x_rows, dkeys, (((0,), (0,)), ((), ())), preferred_elemen...  7.99 us
    gather x1, local copies, waits for them, and re-layouts, per_device(): cot_rows = pool_cot.at[picked].get(mode='promise_in_bounds')  7.7 us
  transfers between devices with their start and end apart: 30, of which 12 were waited for; matrix products, arithmetic and copies ran while one was open for 36% of the time, Pallas kernels for 0%

profile of v5, /device:TPU:0, one launch (start us, length us, event | category | flops | bytes accessed | tf_op | source)
XLA Modules:
  0.0 185.2 jit_solution(8001488273621132842)
XLA Ops:
  1.8 5.1 %collective-permute-start.15 = (bf16[160,512]{1,0:T(8,128)(2,1)S(1)}, bf16[160,512]{1,0:T(8,128)(2,1)S(1)}, u32[]{:S(2)}, u32[]{:S(2)}) collective-permute-start(bf16[160,512]{1,0:T(8,128)(2,1)S(1)} %get-tuple-element.71), channel_id=1, source_target_pairs={{0,12},{2,14},{4,0},{6,2},{8,4},{10,6},{12,8},{14,10},{1,13},{3,15... | collective-permute-start | bytes 491528 | tf_op jit(solution)/shard_map/ppermute | solution.py:49
  7.9 2.8 %collective-permute-start = (bf16[160,512]{1,0:T(8,128)(2,1)S(1)}, bf16[160,512]{1,0:T(8,128)(2,1)S(1)}, u32[]{:S(2)}, u32[]{:S(2)}) collective-permute-start(bf16[160,512]{1,0:T(8,128)(2,1)S(1)} %get-tuple-element.70), channel_id=1, source_target_pairs={{0,12},{2,14},{4,0},{6,2},{8,4},{10,6},{12,8},{14,10},{1,13},{3,15... | collective-permute-start | bytes 491528 | tf_op jit(solution)/shard_map/ppermute | solution.py:49
  12.8 9.3 %collective-permute-done = bf16[160,512]{1,0:T(8,128)(2,1)S(1)} collective-permute-done((bf16[160,512]{1,0:T(8,128)(2,1)S(1)}, bf16[160,512]{1,0:T(8,128)(2,1)S(1)}, u32[]{:S(2)}, u32[]{:S(2)}) %collective-permute-start) | collective-permute-done | bytes 163872 | tf_op jit(solution)/shard_map/ppermute | solution.py:49
  22.1 12.8 %collective-permute-done.16 = bf16[160,512]{1,0:T(8,128)(2,1)S(1)} collective-permute-done((bf16[160,512]{1,0:T(8,128)(2,1)S(1)}, bf16[160,512]{1,0:T(8,128)(2,1)S(1)}, u32[]{:S(2)}, u32[]{:S(2)}) %collective-permute-start.16) | collective-permute-done | bytes 163872 | tf_op jit(solution)/shard_map/ppermute | solution.py:49
  37.7 15.8 %gather_fusion = bf16[1024,2560]{1,0:T(8,128)(2,1)} fusion(bf16[2048,2560]{1,0:T(8,128)(2,1)} %param.7, s32[1024]{0:T(1024)S(1)} %broadcast_clamp_fusion), kind=kCustom, calls=%fused_computation | custom fusion | bytes 10489856 | tf_op jit(solution)/shard_map/gather | solution.py:103
  57.6 7.7 %gather_fusion.1 = bf16[1024,1024]{1,0:T(8,128)(2,1)S(1)} fusion(bf16[2048,1024]{1,0:T(8,128)(2,1)} %param.8, s32[1024]{0:T(1024)S(1)} %broadcast_clamp_fusion), kind=kCustom, calls=%fused_computation.1 | custom fusion | bytes 4198400 | tf_op jit(solution)/shard_map/gather | solution.py:104
  69.7 8.0 %copy.22 = bf16[2560,1024]{1,0:T(8,128)(2,1)} copy(bf16[2560,1024]{0,1:T(8,128)(2,1)} %bitcast.256) | data formatting | bytes 10485760 | tf_op jit(solution)/shard_map/dot_general | solution.py:117
  79.6 2.8 %fusion.8 = bf16[2,4,2,160,512]{4,3,0,2,1:T(8,128)(2,1)S(1)} fusion(s32[]{:T(128)S(6)} %select_n.97, bf16[1,4,2,160,512]{4,3,0,2,1:T(8,128)(2,1)} %bitcast.12, bf16[1,4,2,160,512]{4,3,0,2,1:T(8,128)(2,1)S(1)} %get-tuple-element.48), kind=kLoop, calls=%fused_computation.16 | loop fusion | flops 2621440 | bytes 5242884 | tf_op jit(solution)/shard_map/stack | solution.py:25
  88.0 1.6 multiply_reduce_fusion.5
  93.5 10.4 %collective-permute-done.5 = bf16[4,320,256]{2,1,0:T(8,128)(2,1)S(1)} collective-permute-done((bf16[4,320,256]{2,1,0:T(8,128)(2,1)S(1)}, bf16[4,320,256]{2,1,0:T(8,128)(2,1)S(1)}, u32[]{:S(2)}, u32[]{:S(2)}) %collective-permute-start.5) | collective-permute-done | bytes 655392 | tf_op jit(solution)/shard_map/ppermute | solution.py:77
  104.2 2.7 %collective-permute-start.8 = (bf16[320,256]{1,0:T(8,128)(2,1)S(1)}, bf16[320,256]{1,0:T(8,128)(2,1)S(1)}, u32[]{:S(2)}, u32[]{:S(2)}) collective-permute-start(bf16[320,256]{1,0:T(8,128)(2,1)S(1)} %get-tuple-element.65), channel_id=1, source_target_pairs={{0,12},{2,14},{4,0},{6,2},{8,4},{10,6},{12,8},{14,10},{1,13},{3,15... | collective-permute-start | bytes 491528 | tf_op jit(solution)/shard_map/ppermute | solution.py:88
  109.0 1.6 multiply_reduce_fusion.3
  113.0 1.6 multiply_reduce_fusion.1
  115.3 8.3 %collective-permute-done.10 = bf16[4,320,256]{2,1,0:T(8,128)(2,1)S(1)} collective-permute-done((bf16[4,320,256]{2,1,0:T(8,128)(2,1)S(1)}, bf16[4,320,256]{2,1,0:T(8,128)(2,1)S(1)}, u32[]{:S(2)}, u32[]{:S(2)}) %collective-permute-start.10) | collective-permute-done | bytes 655392 | tf_op jit(solution)/shard_map/ppermute | solution.py:77
  126.4 1.6 fusion.41
  128.2 3.2 %collective-permute-start.13 = (bf16[320,256]{1,0:T(8,128)(2,1)S(1)}, bf16[320,256]{1,0:T(8,128)(2,1)S(1)}, u32[]{:S(2)}, u32[]{:S(2)}) collective-permute-start(bf16[320,256]{1,0:T(8,128)(2,1)S(1)} %get-tuple-element.62), channel_id=1, source_target_pairs={{0,12},{2,14},{4,0},{6,2},{8,4},{10,6},{12,8},{14,10},{1,13},{3,15... | collective-permute-start | bytes 491528 | tf_op jit(solution)/shard_map/ppermute | solution.py:88
  132.6 7.5 %collective-permute-done.20 = bf16[4,320,256]{2,1,0:T(8,128)(2,1)S(1)} collective-permute-done((bf16[4,320,256]{2,1,0:T(8,128)(2,1)S(1)}, bf16[4,320,256]{2,1,0:T(8,128)(2,1)S(1)}, u32[]{:S(2)}, u32[]{:S(2)}) %collective-permute-start.20) | collective-permute-done | bytes 655392 | tf_op jit(solution)/shard_map/ppermute | solution.py:77
  141.4 3.5 %collective-permute-done.12 = bf16[320,256]{1,0:T(8,128)(2,1)S(1)} collective-permute-done((bf16[320,256]{1,0:T(8,128)(2,1)S(1)}, bf16[320,256]{1,0:T(8,128)(2,1)S(1)}, u32[]{:S(2)}, u32[]{:S(2)}) %collective-permute-start.12) | collective-permute-done | bytes 163872 | tf_op jit(solution)/shard_map/ppermute | solution.py:88
  146.5 3.5 %collective-permute-start.23 = (bf16[320,256]{1,0:T(8,128)(2,1)S(1)}, bf16[320,256]{1,0:T(8,128)(2,1)S(1)}, u32[]{:S(2)}, u32[]{:S(2)}) collective-permute-start(bf16[320,256]{1,0:T(8,128)(2,1)S(1)} %get-tuple-element.57), channel_id=1, source_target_pairs={{0,12},{2,14},{4,0},{6,2},{8,4},{10,6},{12,8},{14,10},{1,13},{3,15... | collective-permute-start | bytes 491528 | tf_op jit(solution)/shard_map/ppermute | solution.py:88
  150.1 10.2 %collective-permute-done.25 = bf16[4,320,256]{2,1,0:T(8,128)(2,1)} collective-permute-done((bf16[4,320,256]{2,1,0:T(8,128)(2,1)S(1)}, bf16[4,320,256]{2,1,0:T(8,128)(2,1)}, u32[]{:S(2)}, u32[]{:S(2)}) %collective-permute-start.25) | collective-permute-done | bytes 655392 | tf_op jit(solution)/shard_map/ppermute | solution.py:77
  160.3 1.7 fusion.67
  163.3 2.6 %collective-permute-start.28 = (bf16[320,256]{1,0:T(8,128)(2,1)S(1)}, bf16[320,256]{1,0:T(8,128)(2,1)S(1)}, u32[]{:S(2)}, u32[]{:S(2)}) collective-permute-start(bf16[320,256]{1,0:T(8,128)(2,1)S(1)} %get-tuple-element.60), channel_id=1, source_target_pairs={{0,12},{2,14},{4,0},{6,2},{8,4},{10,6},{12,8},{14,10},{1,13},{3,15... | collective-permute-start | bytes 491528 | tf_op jit(solution)/shard_map/ppermute | solution.py:88
  168.5 2.6 %collective-permute-done.26 = bf16[320,256]{1,0:T(8,128)(2,1)S(1)} collective-permute-done((bf16[320,256]{1,0:T(8,128)(2,1)S(1)}, bf16[320,256]{1,0:T(8,128)(2,1)S(1)}, u32[]{:S(2)}, u32[]{:S(2)}) %collective-permute-start.26) | collective-permute-done | bytes 163872 | tf_op jit(solution)/shard_map/ppermute | solution.py:88
  171.1 7.1 %collective-permute-done.27 = bf16[320,256]{1,0:T(8,128)(2,1)S(1)} collective-permute-done((bf16[320,256]{1,0:T(8,128)(2,1)S(1)}, bf16[320,256]{1,0:T(8,128)(2,1)S(1)}, u32[]{:S(2)}, u32[]{:S(2)}) %collective-permute-start.27) | collective-permute-done | bytes 163872 | tf_op jit(solution)/shard_map/ppermute | solution.py:88
  (155 shorter events, 49.7 us)
Async XLA Ops:
  6.9 28.1 %collective-permute-start.2 = (bf16[160,512]{1,0:T(8,128)(2,1)S(1)}, bf16[160,512]{1,0:T(8,128)(2,1)S(1)}, u32[]{:S(2)}, u32[]{:S(2)}) collective-permute-start(bf16[160,512]{1,0:T(8,128)(2,1)S(1)} %get-tuple-element.70), channel_id=1, source_target_pairs={{0,4},{2,6},{4,8},{6,10},{8,12},{10,14},{12,0},{14,2},{1,5},{3,7},... | collective-permute-start | bytes 491528 | tf_op jit(solution)/shard_map/ppermute | solution.py:49
  6.9 28.0 %collective-permute-start.1 = (bf16[160,512]{1,0:T(8,128)(2,1)S(1)}, bf16[160,512]{1,0:T(8,128)(2,1)S(1)}, u32[]{:S(2)}, u32[]{:S(2)}) collective-permute-start(bf16[160,512]{1,0:T(8,128)(2,1)S(1)} %get-tuple-element.70), channel_id=1, source_target_pairs={{0,8},{2,10},{4,12},{6,14},{8,0},{10,2},{12,4},{14,6},{1,9},{3,11}... | collective-permute-start | bytes 491528 | tf_op jit(solution)/shard_map/ppermute | solution.py:49
  7.9 14.2 %collective-permute-start = (bf16[160,512]{1,0:T(8,128)(2,1)S(1)}, bf16[160,512]{1,0:T(8,128)(2,1)S(1)}, u32[]{:S(2)}, u32[]{:S(2)}) collective-permute-start(bf16[160,512]{1,0:T(8,128)(2,1)S(1)} %get-tuple-element.70), channel_id=1, source_target_pairs={{0,12},{2,14},{4,0},{6,2},{8,4},{10,6},{12,8},{14,10},{1,13},{3,15... | collective-permute-start | bytes 491528 | tf_op jit(solution)/shard_map/ppermute | solution.py:49
  10.7 24.2 %collective-permute-start.17 = (bf16[160,512]{1,0:T(8,128)(2,1)S(1)}, bf16[160,512]{1,0:T(8,128)(2,1)S(1)}, u32[]{:S(2)}, u32[]{:S(2)}) collective-permute-start(bf16[160,512]{1,0:T(8,128)(2,1)S(1)} %get-tuple-element.71), channel_id=1, source_target_pairs={{0,4},{2,6},{4,8},{6,10},{8,12},{10,14},{12,0},{14,2},{1,5},{3,7},... | collective-permute-start | bytes 491528 | tf_op jit(solution)/shard_map/ppermute | solution.py:49
  11.5 23.4 %collective-permute-start.16 = (bf16[160,512]{1,0:T(8,128)(2,1)S(1)}, bf16[160,512]{1,0:T(8,128)(2,1)S(1)}, u32[]{:S(2)}, u32[]{:S(2)}) collective-permute-start(bf16[160,512]{1,0:T(8,128)(2,1)S(1)} %get-tuple-element.71), channel_id=1, source_target_pairs={{0,8},{2,10},{4,12},{6,14},{8,0},{10,2},{12,4},{14,6},{1,9},{3,11}... | collective-permute-start | bytes 491528 | tf_op jit(solution)/shard_map/ppermute | solution.py:49
  36.2 18.1 %collective-permute-start.3 = (bf16[4,160,512]{2,1,0:T(8,128)(2,1)S(1)}, bf16[4,160,512]{2,1,0:T(8,128)(2,1)S(1)}, u32[]{:S(2)}, u32[]{:S(2)}) collective-permute-start(bf16[4,160,512]{2,1,0:T(8,128)(2,1)S(1)} %constant_dynamic-slice_fusion.1), channel_id=1, source_target_pairs={{0,2},{2,0},{4,6},{6,4},{8,10},{10,8},{12,14},{14,12},{1,3},{3,1},... | collective-permute-start | bytes 1966088 | tf_op jit(solution)/shard_map/ppermute | solution.py:53
  55.6 24.0 %collective-permute-start.4 = (bf16[4,2,160,512]{3,2,1,0:T(8,128)(2,1)}, bf16[4,2,160,512]{3,2,1,0:T(8,128)(2,1)}, u32[]{:S(2)}, u32[]{:S(2)}) collective-permute-start(bf16[4,2,160,512]{3,2,1,0:T(8,128)(2,1)} %get-tuple-element.49), channel_id=1, source_target_pairs={{0,1},{1,0},{2,3},{3,2},{4,5},{5,4},{6,7},{7,6},{8,9},{9,8},{10,11... | collective-permute-start | bytes 3932168 | tf_op jit(solution)/shard_map/ppermute | solution.py:60
  57.0 20.7 %collective-permute-start.18 = (bf16[4,160,512]{2,1,0:T(8,128)(2,1)}, bf16[4,160,512]{2,1,0:T(8,128)(2,1)}, u32[]{:S(2)}, u32[]{:S(2)}) collective-permute-start(bf16[4,160,512]{2,1,0:T(8,128)(2,1)} %constant_dynamic-slice_fusion), channel_id=1, source_target_pairs={{0,2},{2,0},{4,6},{6,4},{8,10},{10,8},{12,14},{14,12},{1,3},{3,1},... | collective-permute-start | bytes 1966088 | tf_op jit(solution)/shard_map/ppermute | solution.py:53
  79.5 12.5 %collective-permute-start.19 = (bf16[4,2,160,512]{3,2,0,1:T(8,128)(2,1)S(1)}, bf16[4,2,160,512]{3,2,0,1:T(8,128)(2,1)S(1)}, u32[]{:S(2)}, u32[]{:S(2)}) collective-permute-start(bf16[4,2,160,512]{3,2,0,1:T(8,128)(2,1)S(1)} %get-tuple-element.53), channel_id=1, source_target_pairs={{0,1},{1,0},{2,3},{3,2},{4,5},{5,4},{6,7},{7,6},{8,9},{9,8},{10,11... | collective-permute-start | bytes 3932168 | tf_op jit(solution)/shard_map/ppermute | solution.py:60
  86.4 17.6 %collective-permute-start.5 = (bf16[4,320,256]{2,1,0:T(8,128)(2,1)S(1)}, bf16[4,320,256]{2,1,0:T(8,128)(2,1)S(1)}, u32[]{:S(2)}, u32[]{:S(2)}) collective-permute-start(bf16[4,320,256]{2,1,0:T(8,128)(2,1)S(1)} %fusion.37), channel_id=1, source_target_pairs={{0,2},{2,0},{4,6},{6,4},{8,10},{10,8},{12,14},{14,12},{1,3},{3,1},... | collective-permute-start | bytes 1966088 | tf_op jit(solution)/shard_map/ppermute | solution.py:77
  104.2 20.7 %collective-permute-start.8 = (bf16[320,256]{1,0:T(8,128)(2,1)S(1)}, bf16[320,256]{1,0:T(8,128)(2,1)S(1)}, u32[]{:S(2)}, u32[]{:S(2)}) collective-permute-start(bf16[320,256]{1,0:T(8,128)(2,1)S(1)} %get-tuple-element.65), channel_id=1, source_target_pairs={{0,12},{2,14},{4,0},{6,2},{8,4},{10,6},{12,8},{14,10},{1,13},{3,15... | collective-permute-start | bytes 491528 | tf_op jit(solution)/shard_map/ppermute | solution.py:88
  106.9 18.0 %collective-permute-start.7 = (bf16[320,256]{1,0:T(8,128)(2,1)S(1)}, bf16[320,256]{1,0:T(8,128)(2,1)S(1)}, u32[]{:S(2)}, u32[]{:S(2)}) collective-permute-start(bf16[320,256]{1,0:T(8,128)(2,1)S(1)} %get-tuple-element.66), channel_id=1, source_target_pairs={{0,8},{2,10},{4,12},{6,14},{8,0},{10,2},{12,4},{14,6},{1,9},{3,11}... | collective-permute-start | bytes 491528 | tf_op jit(solution)/shard_map/ppermute | solution.py:88
  106.9 18.0 %collective-permute-start.6 = (bf16[320,256]{1,0:T(8,128)(2,1)S(1)}, bf16[320,256]{1,0:T(8,128)(2,1)S(1)}, u32[]{:S(2)}, u32[]{:S(2)}) collective-permute-start(bf16[320,256]{1,0:T(8,128)(2,1)S(1)} %get-tuple-element.67), channel_id=1, source_target_pairs={{0,4},{2,6},{4,8},{6,10},{8,12},{10,14},{12,0},{14,2},{1,5},{3,7},... | collective-permute-start | bytes 491528 | tf_op jit(solution)/shard_map/ppermute | solution.py:88
  107.5 16.1 %collective-permute-start.10 = (bf16[4,320,256]{2,1,0:T(8,128)(2,1)S(1)}, bf16[4,320,256]{2,1,0:T(8,128)(2,1)S(1)}, u32[]{:S(2)}, u32[]{:S(2)}) collective-permute-start(bf16[4,320,256]{2,1,0:T(8,128)(2,1)S(1)} %fusion.38), channel_id=1, source_target_pairs={{0,2},{2,0},{4,6},{6,4},{8,10},{10,8},{12,14},{14,12},{1,3},{3,1},... | collective-permute-start | bytes 1966088 | tf_op jit(solution)/shard_map/ppermute | solution.py:77
  124.9 15.2 %collective-permute-start.20 = (bf16[4,320,256]{2,1,0:T(8,128)(2,1)S(1)}, bf16[4,320,256]{2,1,0:T(8,128)(2,1)S(1)}, u32[]{:S(2)}, u32[]{:S(2)}) collective-permute-start(bf16[4,320,256]{2,1,0:T(8,128)(2,1)S(1)} %fusion.39), channel_id=1, source_target_pairs={{0,2},{2,0},{4,6},{6,4},{8,10},{10,8},{12,14},{14,12},{1,3},{3,1},... | collective-permute-start | bytes 1966088 | tf_op jit(solution)/shard_map/ppermute | solution.py:77
  128.2 13.1 %collective-permute-start.13 = (bf16[320,256]{1,0:T(8,128)(2,1)S(1)}, bf16[320,256]{1,0:T(8,128)(2,1)S(1)}, u32[]{:S(2)}, u32[]{:S(2)}) collective-permute-start(bf16[320,256]{1,0:T(8,128)(2,1)S(1)} %get-tuple-element.62), channel_id=1, source_target_pairs={{0,12},{2,14},{4,0},{6,2},{8,4},{10,6},{12,8},{14,10},{1,13},{3,15... | collective-permute-start | bytes 491528 | tf_op jit(solution)/shard_map/ppermute | solution.py:88
  131.5 13.4 %collective-permute-start.12 = (bf16[320,256]{1,0:T(8,128)(2,1)S(1)}, bf16[320,256]{1,0:T(8,128)(2,1)S(1)}, u32[]{:S(2)}, u32[]{:S(2)}) collective-permute-start(bf16[320,256]{1,0:T(8,128)(2,1)S(1)} %get-tuple-element.63), channel_id=1, source_target_pairs={{0,8},{2,10},{4,12},{6,14},{8,0},{10,2},{12,4},{14,6},{1,9},{3,11}... | collective-permute-start | bytes 491528 | tf_op jit(solution)/shard_map/ppermute | solution.py:88
  132.3 12.6 %collective-permute-start.11 = (bf16[320,256]{1,0:T(8,128)(2,1)S(1)}, bf16[320,256]{1,0:T(8,128)(2,1)S(1)}, u32[]{:S(2)}, u32[]{:S(2)}) collective-permute-start(bf16[320,256]{1,0:T(8,128)(2,1)S(1)} %get-tuple-element.64), channel_id=1, source_target_pairs={{0,4},{2,6},{4,8},{6,10},{8,12},{10,14},{12,0},{14,2},{1,5},{3,7},... | collective-permute-start | bytes 491528 | tf_op jit(solution)/shard_map/ppermute | solution.py:88
  145.6 14.7 %collective-permute-start.25 = (bf16[4,320,256]{2,1,0:T(8,128)(2,1)S(1)}, bf16[4,320,256]{2,1,0:T(8,128)(2,1)}, u32[]{:S(2)}, u32[]{:S(2)}) collective-permute-start(bf16[4,320,256]{2,1,0:T(8,128)(2,1)S(1)} %fusion.40), channel_id=1, source_target_pairs={{0,2},{2,0},{4,6},{6,4},{8,10},{10,8},{12,14},{14,12},{1,3},{3,1},... | collective-permute-start | bytes 1966088 | tf_op jit(solution)/shard_map/ppermute | solution.py:77
  146.2 19.8 %collective-permute-start.21 = (bf16[320,256]{1,0:T(8,128)(2,1)S(1)}, bf16[320,256]{1,0:T(8,128)(2,1)S(1)}, u32[]{:S(2)}, u32[]{:S(2)}) collective-permute-start(bf16[320,256]{1,0:T(8,128)(2,1)S(1)} %get-tuple-element.56), channel_id=1, source_target_pairs={{0,4},{2,6},{4,8},{6,10},{8,12},{10,14},{12,0},{14,2},{1,5},{3,7},... | collective-permute-start | bytes 491528 | tf_op jit(solution)/shard_map/ppermute | solution.py:88
  146.5 21.8 %collective-permute-start.23 = (bf16[320,256]{1,0:T(8,128)(2,1)S(1)}, bf16[320,256]{1,0:T(8,128)(2,1)S(1)}, u32[]{:S(2)}, u32[]{:S(2)}) collective-permute-start(bf16[320,256]{1,0:T(8,128)(2,1)S(1)} %get-tuple-element.57), channel_id=1, source_target_pairs={{0,12},{2,14},{4,0},{6,2},{8,4},{10,6},{12,8},{14,10},{1,13},{3,15... | collective-permute-start | bytes 491528 | tf_op jit(solution)/shard_map/ppermute | solution.py:88
  150.1 18.4 %collective-permute-start.22 = (bf16[320,256]{1,0:T(8,128)(2,1)S(1)}, bf16[320,256]{1,0:T(8,128)(2,1)S(1)}, u32[]{:S(2)}, u32[]{:S(2)}) collective-permute-start(bf16[320,256]{1,0:T(8,128)(2,1)S(1)} %get-tuple-element.58), channel_id=1, source_target_pairs={{0,8},{2,10},{4,12},{6,14},{8,0},{10,2},{12,4},{14,6},{1,9},{3,11}... | collective-permute-start | bytes 491528 | tf_op jit(solution)/shard_map/ppermute | solution.py:88
  166.0 12.3 %collective-permute-start.27 = (bf16[320,256]{1,0:T(8,128)(2,1)S(1)}, bf16[320,256]{1,0:T(8,128)(2,1)S(1)}, u32[]{:S(2)}, u32[]{:S(2)}) collective-permute-start(bf16[320,256]{1,0:T(8,128)(2,1)S(1)} %get-tuple-element.61), channel_id=1, source_target_pairs={{0,8},{2,10},{4,12},{6,14},{8,0},{10,2},{12,4},{14,6},{1,9},{3,11}... | collective-permute-start | bytes 491528 | tf_op jit(solution)/shard_map/ppermute | solution.py:88
  168.4 13.0 %collective-permute-start.14 = (f32[320,256]{1,0:T(8,128)S(1)}, f32[320,256]{1,0:T(8,128)S(1)}, u32[]{:S(2)}, u32[]{:S(2)}) collective-permute-start(f32[320,256]{1,0:T(8,128)S(1)} %get-tuple-element.19), channel_id=1, source_target_pairs={{0,1},{1,0},{2,3},{3,2},{4,5},{5,4},{6,7},{7,6},{8,9},{9,8},{10,11... | collective-permute-start | bytes 983048 | tf_op jit(solution)/shard_map/ppermute | solution.py:130
  (28 other events, 157.4 us)
